TPU v7x, 32 devices: a whole 2x2x4 slice. The times are simulated.
32 devices in a mesh: groups: 2 (over y), gx: 4 (over z), gy: 2 (over x), lev: 2 (over core).
Axes of the slice: x: 2, y: 2, z: 4, core: 2. Of those that a mesh axis runs over, the one named last changes fastest.
Arguments:
- anomaly_codes: bfloat16 [40, 4, 128, 256], P(None, 'lev', ('groups', 'gx'), 'gy'), parts along dimension 2, may hold values from -127 to 127
- block_scales: float32 [40, 4, 128, 2], P(None, 'lev', ('groups', 'gx'), 'gy'), parts along dimension 2, may hold values from 0.004 to 0.04
- background: float32 [4, 128, 256], P('lev', ('groups', 'gx'), 'gy'), parts along dimension 1, may hold values from -6 to 6
- obs_values: float32 [8, 2, 128], P(('groups', 'gx'), 'gy'), parts along dimension 0, may hold values from -12 to 12
- obs_error: float32 [8, 2, 128], P(('groups', 'gx'), 'gy'), parts along dimension 0, may hold values from 0.2 to 2
- obs_cell: int32 [8, 2, 128], P(('groups', 'gx'), 'gy'), parts along dimension 0, may hold values from 0 to 2047
- obs_level: int32 [8, 2, 128], P(('groups', 'gx'), 'gy'), parts along dimension 0, may hold values from 0 to 3
- obs_count: int32 [8, 2], P(('groups', 'gx'), 'gy'), parts along dimension 0, may hold values from 64 to 128, as said below
- conv1_weight: float32 [3, 3, 8, 32], replicated, may hold values from -0.75 to 0.75
- conv1_bias: float32 [32], replicated, may hold values from -3 to 3
- conv2_weight: float32 [3, 3, 32, 32], replicated, may hold values from -0.375 to 0.375
- conv2_bias: float32 [32], replicated, may hold values from -3 to 3
- head_weight: float32 [32], replicated, may hold values from -1 to 1
- head_bias: float32 [1], replicated, may hold values from -3 to 3
Outputs:
- increment: float32 [4, 128, 256], P('lev', ('groups', 'gx'), 'gy'), parts along dimension 1
- taper_field: float32 [128, 256], P(('groups', 'gx'), 'gy'), parts along dimension 0
There are 2 independent parts, one for each index of `groups`. A program takes and returns all parts, laid end to end along the dimension named above; an argument that names none is the same for every part. Nothing has to cross between parts.
Inputs may be any that keep to these rules, and one draw needn't show every extreme that they name: `obs_count`: in every draw at least one tile uses all 128 slots.
All inputs are finite; a program needn't handle non-finite values.
Results may differ from a plain program's by a relative error of at most 0.0003.
The roundings to bfloat16 on the way count: a program that leaves them out, or rounds other values in their place, can miss the bound.
Values may be sent and summed in bfloat16 or wider, within the bound.
A program may use at most 64 MiB of HBM per device.

v0:
```python
import math

import jax
import jax.numpy as jnp
from jax import lax
from jax.sharding import PartitionSpec as P

STEP = 2
VCUT = 6
CUT = 6


unit_moves = ((-1, -1), (-1, 0), (-1, 1), (0, -1), (0, 1), (1, -1), (1, 0), (1, 1))
epsilon = 1e-06
highest = lax.Precision.HIGHEST


def extended(x, sides, width):
    for axis, dim in sides:
        devices, length = (lax.axis_size(axis), x.shape[dim])
        up = [(i, (i + 1) % devices) for i in range(devices - 1)]
        down = [(j, i) for i, j in up]
        last = lax.slice_in_dim(x, length - width, length, axis=dim)
        initial = lax.slice_in_dim(x, 0, width, axis=dim)
        before = lax.ppermute(last, axis, up)
        after = lax.ppermute(initial, axis, down)
        x = jnp.concatenate([before, x, after], axis=dim)
    return x


def dequantize(anomaly_codes, block_scales):
    members, lev_dev, tile_rows, tile_cols = anomaly_codes.shape
    blocked = anomaly_codes.reshape(members, lev_dev, tile_rows, tile_cols // 128, 128).astype(
        jnp.float32
    )
    return (blocked * block_scales[..., None]).reshape(members, lev_dev, tile_rows, tile_cols)


def valid_conv(inputs, kernel):
    return lax.conv_general_dilated(
        inputs[None],
        kernel,
        (1, 1),
        "VALID",
        dimension_numbers=("NCHW", "HWIO", "NCHW"),
        precision=highest,
    )[0]


def vertical_taper(level_one, level_two):
    ratio = (level_one - level_two) / VCUT
    return jnp.square(jnp.maximum(0.0, 1.0 - ratio * ratio))


def local_sums(padded, weight_total):
    squares = jnp.sum(padded * padded, axis=(0, 1)) / weight_total
    inner_rows = padded.shape[2] - 2 * STEP
    inner_cols = padded.shape[3] - 2 * STEP
    centre = padded[:, :, STEP : STEP + inner_rows, STEP : STEP + inner_cols]
    product_list = []
    for offset in unit_moves:
        row_from = STEP + offset[0] * STEP
        col_from = STEP + offset[1] * STEP
        shifted = padded[:, :, row_from : row_from + inner_rows, col_from : col_from + inner_cols]
        product_list.append(jnp.sum(centre * shifted, axis=(0, 1)) / weight_total)
    return (squares, jnp.stack(product_list))


def correlate(squares, products):
    inner_rows = products.shape[1]
    inner_cols = products.shape[2]
    centre = squares[STEP : STEP + inner_rows, STEP : STEP + inner_cols]
    channels = []
    for position, offset in enumerate(unit_moves):
        row_from = STEP + offset[0] * STEP
        col_from = STEP + offset[1] * STEP
        shifted = squares[row_from : row_from + inner_rows, col_from : col_from + inner_cols]
        channels.append(products[position] / jnp.sqrt((centre + epsilon) * (shifted + epsilon)))
    return jnp.stack(channels)


def per_device(
    anomaly_codes,
    block_scales,
    background,
    obs_values,
    obs_error,
    obs_cell,
    obs_level,
    obs_count,
    conv1_weight,
    conv1_bias,
    conv2_weight,
    conv2_bias,
    head_weight,
    head_bias,
):
    members, lev_dev, tile_rows, tile_cols = anomaly_codes.shape
    obs_tile = obs_cell.shape[2]
    levels = lev_dev * lax.axis_size("lev")
    weight_total = float(members * levels)
    grid_rows_total = tile_rows * lax.axis_size("gx")
    grid_cols_total = tile_cols * lax.axis_size("gy")
    row_tile = lax.axis_index("gx")
    col_tile = lax.axis_index("gy")
    first_level = lax.axis_index("lev") * lev_dev
    anomalies = dequantize(anomaly_codes, block_scales)
    rim_width = STEP + 2
    padded = extended(anomalies, (("gx", 2), ("gy", 3)), rim_width)
    squares, products = local_sums(padded, weight_total)
    cell_index = obs_cell[0, 0]
    level_index = obs_level[0, 0]
    held_here = (level_index >= first_level) & (level_index < first_level + lev_dev)
    flat_index = jnp.where(
        held_here, (level_index - first_level) * (tile_rows * tile_cols) + cell_index, 0
    )
    picked = jnp.take(
        anomalies.reshape(members, lev_dev * tile_rows * tile_cols), flat_index, axis=1
    )
    own_anom = jnp.where(held_here[None, :], picked, 0.0)
    own_mean = jnp.where(held_here, jnp.take(background.reshape(-1), flat_index), 0.0)
    usable = jnp.arange(obs_tile) < obs_count[0, 0]
    values_here = obs_values[0, 0]
    errors_here = obs_error[0, 0]
    squares, products, obs_anom, obs_mean = lax.psum((squares, products, own_anom, own_mean), "lev")
    misfit = values_here - obs_mean
    spread = jnp.sum(obs_anom * obs_anom, axis=0) / (members - 1)
    statistics = lax.psum(
        (
            jnp.sum(jnp.where(usable, misfit * misfit, 0.0)),
            jnp.sum(jnp.where(usable, spread, 0.0)),
            jnp.sum(jnp.where(usable, errors_here, 0.0)),
        ),
        ("gx", "gy"),
    )
    features = correlate(squares, products)
    hidden = jax.nn.relu(valid_conv(features, conv1_weight) + conv1_bias[:, None, None])
    row_cells = row_tile * tile_rows - 1 + jnp.arange(tile_rows + 2)
    col_cells = col_tile * tile_cols - 1 + jnp.arange(tile_cols + 2)
    inside = ((row_cells >= 0) & (row_cells < grid_rows_total))[:, None] & (
        (col_cells >= 0) & (col_cells < grid_cols_total)
    )[None, :]
    hidden = jnp.where(inside[None], hidden, 0.0)
    hidden = jax.nn.relu(valid_conv(hidden, conv2_weight) + conv2_bias[:, None, None])
    taper_field = jax.nn.sigmoid(
        jnp.einsum("cxy,c->xy", hidden, head_weight, precision=highest) + head_bias[0]
    )
    inflation = statistics[0] / (statistics[1] + statistics[2])
    obs_gain = jnp.where(usable, misfit / (inflation * spread + errors_here), 0.0)
    obs_weight = jnp.take(taper_field.reshape(-1), cell_index) * obs_gain / (members - 1)
    local_rows = cell_index // tile_cols
    local_cols = cell_index % tile_cols
    level_values = (first_level + jnp.arange(lev_dev)).astype(jnp.float32)
    packed = jnp.concatenate(
        [
            obs_anom,
            obs_weight[None],
            level_index.astype(jnp.float32)[None],
            local_rows.astype(jnp.float32)[None],
            local_cols.astype(jnp.float32)[None],
        ],
        0,
    )[None, None]
    beside_all = extended(packed, (("gx", 0), ("gy", 1)), 1)
    near_anom = beside_all[:, :, :members]
    near_weight = beside_all[:, :, members]
    vertical = vertical_taper(
        level_values[:, None, None, None], beside_all[:, :, members + 1][None]
    )
    coefficients = ((vertical * near_weight[None])[:, :, :, None, :] * near_anom[None]).astype(
        jnp.bfloat16
    )
    coeff_matrix = coefficients.transpose(1, 2, 4, 0, 3).reshape(9 * obs_tile, lev_dev * members)
    near_rows = beside_all[:, :, members + 2]
    near_cols = beside_all[:, :, members + 3]
    shift_three = (jnp.arange(3) - 1).astype(jnp.float32)
    obs_rows = (near_rows + shift_three[:, None, None] * tile_rows).reshape(-1)
    obs_cols = (near_cols + shift_three[None, :, None] * tile_cols).reshape(-1)
    row_span = math.gcd(tile_rows, max(1, 1024 // tile_cols))
    group_total = tile_rows // row_span

    def update(group_index):
        row_start = group_index * row_span
        cell_rows = (row_start + jnp.arange(row_span * tile_cols) // tile_cols).astype(jnp.float32)
        cell_cols = (jnp.arange(row_span * tile_cols) % tile_cols).astype(jnp.float32)
        row_gap = cell_rows[:, None] - obs_rows[None, :]
        col_gap = cell_cols[:, None] - obs_cols[None, :]
        distance = row_gap * row_gap + col_gap * col_gap
        localization = jnp.square(jnp.maximum(0.0, 1.0 - distance / (CUT * CUT))).astype(
            jnp.bfloat16
        )
        weights = jnp.dot(localization, coeff_matrix, preferred_element_type=jnp.float32).reshape(
            row_span * tile_cols, lev_dev, members
        )
        slab_anom = lax.dynamic_slice_in_dim(anomalies, row_start, row_span, 2).reshape(
            members, lev_dev, row_span * tile_cols
        )
        combined = jnp.einsum("mlc,clm->lc", slab_anom, weights, precision=highest)
        taper_rows = lax.dynamic_slice_in_dim(taper_field, row_start, row_span, 0).reshape(
            row_span * tile_cols
        )
        return (inflation * taper_rows * combined).reshape(lev_dev, row_span, tile_cols)

    pieces = lax.map(update, jnp.arange(group_total))
    increment = pieces.transpose(1, 0, 2, 3).reshape(lev_dev, tile_rows, tile_cols)
    return (increment, taper_field)


def solution(mesh):
    in_specs = (
        P(None, "lev", ("groups", "gx"), "gy"),
        P(None, "lev", ("groups", "gx"), "gy"),
        P("lev", ("groups", "gx"), "gy"),
        P(("groups", "gx"), "gy", None),
        P(("groups", "gx"), "gy", None),
        P(("groups", "gx"), "gy", None),
        P(("groups", "gx"), "gy", None),
        P(("groups", "gx"), "gy"),
        P(),
        P(),
        P(),
        P(),
        P(),
        P(),
    )
    out_specs = (P("lev", ("groups", "gx"), "gy"), P(("groups", "gx"), "gy"))
    return jax.shard_map(
        per_device, mesh=mesh, in_specs=in_specs, out_specs=out_specs, check_vma=False
    )
```

profile of v0, /device:TPU:0, one launch (start us, length us, event | category | flops | bytes accessed | tf_op | source)
XLA Modules:
  0.0 126.9 jit_solution(7264684300521917502)
XLA Ops:
  10.0 5.1 %collective-permute-start = (f32[40,2,4,128]{3,2,1,0:T(4,128)}, f32[40,2,4,128]{3,2,1,0:T(4,128)S(1)}, u32[]{:S(2)}, u32[]{:S(2)}) collective-permute-start(f32[40,2,4,128]{3,2,1,0:T(4,128)} %get-tuple-element.241), channel_id=1, source_target_pairs={{0,4},{4,8},{8,12},{1,5},{5,9},{9,13},{2,6},{6,10},{10,14},{3,7},{... | collective-permute-start | bytes 491528 | tf_op jit(solution)/shard_map/ppermute | solution.py:25
  15.1 1.3 %collective-permute-start.1 = (f32[40,2,4,128]{3,2,1,0:T(4,128)S(1)}, f32[40,2,4,128]{3,2,1,0:T(4,128)S(1)}, u32[]{:S(2)}, u32[]{:S(2)}) collective-permute-start(f32[40,2,4,128]{3,2,1,0:T(4,128)S(1)} %get-tuple-element.242), channel_id=1, source_target_pairs={{4,0},{8,4},{12,8},{5,1},{9,5},{13,9},{6,2},{10,6},{14,10},{7,3},{... | collective-permute-start | bytes 491528 | tf_op jit(solution)/shard_map/ppermute | solution.py:26
  20.4 2.2 %collective-permute-done.1 = f32[40,2,4,128]{3,2,1,0:T(4,128)S(1)} collective-permute-done((f32[40,2,4,128]{3,2,1,0:T(4,128)S(1)}, f32[40,2,4,128]{3,2,1,0:T(4,128)S(1)}, u32[]{:S(2)}, u32[]{:S(2)}) %collective-permute-start.1) | collective-permute-done | bytes 163872 | tf_op jit(solution)/shard_map/ppermute | solution.py:26
  23.6 3.4 %collective-permute-start.2 = (f32[40,2,24,4]{0,2,3,1:T(8,128)S(1)}, f32[40,2,24,4]{0,2,3,1:T(8,128)S(1)}, u32[]{:S(2)}, u32[]{:S(2)}) collective-permute-start(f32[40,2,24,4]{0,2,3,1:T(8,128)S(1)} %copy.219), channel_id=1, source_target_pairs={{0,2},{1,3},{4,6},{5,7},{8,10},{9,11},{12,14},{13,15},{16,18},{17,... | collective-permute-start | bytes 92168 | tf_op jit(solution)/shard_map/ppermute | solution.py:25
  27.5 1.3 %collective-permute-start.3 = (f32[40,2,24,4]{0,2,3,1:T(8,128)S(1)}, f32[40,2,24,4]{0,2,3,1:T(8,128)S(1)}, u32[]{:S(2)}, u32[]{:S(2)}) collective-permute-start(f32[40,2,24,4]{0,2,3,1:T(8,128)S(1)} %copy.220), channel_id=1, source_target_pairs={{2,0},{3,1},{6,4},{7,5},{10,8},{11,9},{14,12},{15,13},{18,16},{19,... | collective-permute-start | bytes 92168 | tf_op jit(solution)/shard_map/ppermute | solution.py:26
  29.9 4.0 %collective-permute-done.3 = f32[40,2,24,4]{0,2,3,1:T(8,128)S(1)} collective-permute-done((f32[40,2,24,4]{0,2,3,1:T(8,128)S(1)}, f32[40,2,24,4]{0,2,3,1:T(8,128)S(1)}, u32[]{:S(2)}, u32[]{:S(2)}) %collective-permute-start.3) | collective-permute-done | bytes 30752 | tf_op jit(solution)/shard_map/ppermute | solution.py:26
  36.9 2.6 %fusion.16 = (f32[20,132]{1,0:T(8,128)S(1)}, f32[20,132]{1,0:T(8,128)S(1)}, f32[20,132]{1,0:T(8,128)S(1)}, f32[20,132]{1,0:T(8,128)S(1)}, f32[20,132]{1,0:T(8,12...) fusion(f32[40,2,24,132]{3,2,1,0:T(8,128)S(1)} %get-tuple-element.238, ...), kind=kLoop, calls=%fused_computation.30 | loop fusion | flops 3358080 | bytes 7687680 | tf_op jit(solution)/shard_map/reduce_sum | solution.py:65
  41.4 3.7 %all-reduce.1 = (f32[128]{0:T(128)S(1)}, f32[40,128]{0,1:T(8,128)S(1)}, f32[24,136]{0,1:T(8,128)S(1)}) all-reduce(f32[128]{0:T(128)S(1)} %get-tuple-element.231, f32[40,128]{0,1:T(8,128)S(1)} %select_bitcast_fusion, f32[24,136]{0,1:T(8,128)S(1)} %broadcast_multiply_fusion), channel_id=1, replica_groups=mesh['groups'=2,'gx'=4,'gy'=2,'lev'=2] {'lev'}, use_global_device_ids=true, to_apply=%region_12.13 | all-reduce | flops 8512 | bytes 68096 | tf_op jit(solution)/shard_map/psum | solution.py:125
  47.2 19.3 %all-reduce = (f32[]{:T(128)}, f32[]{:T(128)}) all-reduce(f32[]{:T(128)} %get-tuple-element.258, f32[]{:T(128)S(6)} %add.277), channel_id=1, replica_groups=mesh['groups'=2,'gx'=4,'gy'=2,'lev'=2] {'gx','gy'}, use_global_device_ids=true, to_apply=%region_15.16 | all-reduce | flops 2 | bytes 16 | tf_op jit(solution)/shard_map/psum | solution.py:128
  72.5 6.4 %fusion.43 = f32[18,8,17,32]{3,1,2,0:T(8,128)} fusion(f32[3,3,8,32]{3,2,1,0:T(8,128)S(1)} %copy-done.10, f32[8,20,1,7,2]{0,3,4,1,2:T(8,128)S(1)} %slice.186, f32[8,20,1,8,17]{0,3,4,1,2:T(8,128)S(1)} %copy.189, f32[32]{0:T(128)S(1)} %copy-done.11, pred[8,17]{0,1:T(8,128)(4,1)S(1)} %copy-done.13), kind=kOutput, calls=%fused_computation.64 | convolution fusion | flops 67990272 | bytes 418824 | tf_op jit(solution)/shard_map/conv_general_dilated | solution.py:40
  78.9 2.2 %copy.190 = f32[18,8,17,32]{2,1,3,0:T(8,128)S(1)} copy(f32[18,8,17,32]{3,1,2,0:T(8,128)} %fusion.43) | data formatting | bytes 626688 | tf_op jit(solution)/shard_map/jit(relu)/max | solution.py:137
  81.1 1.4 %reshape.479 = f32[18,1,136,32]{2,3,0,1:T(8,128)} reshape(f32[18,8,17,32]{2,1,3,0:T(8,128)S(1)} %copy.190) | data formatting | bytes 626688 | tf_op jit(solution)/shard_map/jit(relu)/max | solution.py:137
  83.7 2.1 %copy.221 = f32[32,18,1,130]{0,2,3,1:T(1,128)S(1)} copy(f32[32,18,1,130]{3,0,1,2:T(8,128)S(1)} %fusion.54) | data formatting | bytes 599040
  87.3 5.1 %fusion.37 = f32[16,8,17,32]{3,1,2,0:T(8,128)S(1)} fusion(f32[3,3,32,32]{3,2,1,0:T(8,128)S(1)} %copy-done, f32[32,18,1,7,2]{0,3,4,1,2:T(8,128)S(1)} %slice.188, f32[32,18,1,8,17]{0,3,4,1,2:T(8,128)S(1)} %copy.193, pred[8,17]{0,1:T(8,128)(4,1)S(1)} %copy-done.12), kind=kOutput, calls=%fused_computation.62 | convolution fusion | flops 240980480 | bytes 661128 | tf_op jit(solution)/shard_map/conv_general_dilated | solution.py:40
  93.1 1.3 %fusion.48 = f32[1,16,128]{2,0,1:T(1,128)S(1)} fusion(f32[32,16,128]{0,1,2:T(8,128)S(1)} %fusion.47, f32[32]{0:T(128)S(1)} %copy-done.8), kind=kOutput, calls=%fused_computation.68 | convolution fusion | flops 786432 | bytes 270464 | tf_op jit(solution)/shard_map/cxy,c->xy/dot_general | solution.py:146
  95.7 1.3 %collective-permute-start.4 = (f32[1,1,44,128]{3,2,1,0:T(8,128)S(1)}, f32[1,1,44,128]{3,2,1,0:T(8,128)S(1)}, u32[]{:S(2)}, u32[]{:S(2)}) collective-permute-start(f32[1,1,44,128]{3,2,1,0:T(8,128)S(1)} %bitcast.252), channel_id=1, source_target_pairs={{0,4},{4,8},{8,12},{1,5},{5,9},{9,13},{2,6},{6,10},{10,14},{3,7},{... | collective-permute-start | bytes 67592 | tf_op jit(solution)/shard_map/ppermute | solution.py:25
  97.0 1.3 %collective-permute-start.5 = (f32[1,1,44,128]{3,2,1,0:T(8,128)S(1)}, f32[1,1,44,128]{3,2,1,0:T(8,128)S(1)}, u32[]{:S(2)}, u32[]{:S(2)}) collective-permute-start(f32[1,1,44,128]{3,2,1,0:T(8,128)S(1)} %bitcast.253), channel_id=1, source_target_pairs={{4,0},{8,4},{12,8},{5,1},{9,5},{13,9},{6,2},{10,6},{14,10},{7,3},{... | collective-permute-start | bytes 67592 | tf_op jit(solution)/shard_map/ppermute | solution.py:26
  98.5 4.2 %collective-permute-done.5 = f32[1,1,44,128]{3,2,1,0:T(8,128)S(1)} collective-permute-done((f32[1,1,44,128]{3,2,1,0:T(8,128)S(1)}, f32[1,1,44,128]{3,2,1,0:T(8,128)S(1)}, u32[]{:S(2)}, u32[]{:S(2)}) %collective-permute-start.5) | collective-permute-done | bytes 22560 | tf_op jit(solution)/shard_map/ppermute | solution.py:26
  102.7 2.4 %collective-permute-start.6 = (f32[3,1,44,128]{3,2,1,0:T(8,128)S(1)}, f32[3,1,44,128]{3,2,1,0:T(8,128)S(1)}, u32[]{:S(2)}, u32[]{:S(2)}) collective-permute-start(f32[3,1,44,128]{3,2,1,0:T(8,128)S(1)} %pad_maximum_fusion.4), channel_id=1, source_target_pairs={{0,2},{1,3},{4,6},{5,7},{8,10},{9,11},{12,14},{13,15},{16,18},{17,... | collective-permute-start | bytes 202760 | tf_op jit(solution)/shard_map/ppermute | solution.py:25
  105.1 1.3 %collective-permute-start.7 = (f32[3,1,44,128]{3,2,1,0:T(8,128)S(1)}, f32[3,1,44,128]{3,2,1,0:T(8,128)S(1)}, u32[]{:S(2)}, u32[]{:S(2)}) collective-permute-start(f32[3,1,44,128]{3,2,1,0:T(8,128)S(1)} %pad_maximum_fusion.4), channel_id=1, source_target_pairs={{2,0},{3,1},{6,4},{7,5},{10,8},{11,9},{14,12},{15,13},{18,16},{19,... | collective-permute-start | bytes 202760 | tf_op jit(solution)/shard_map/ppermute | solution.py:26
  107.1 4.3 %collective-permute-done.7 = f32[3,1,44,128]{3,2,1,0:T(8,128)S(1)} collective-permute-done((f32[3,1,44,128]{3,2,1,0:T(8,128)S(1)}, f32[3,1,44,128]{3,2,1,0:T(8,128)S(1)}, u32[]{:S(2)}, u32[]{:S(2)}) %collective-permute-start.7) | collective-permute-done | bytes 67616 | tf_op jit(solution)/shard_map/ppermute | solution.py:26
  111.7 7.7 %while.13 = (s32[]{:T(128)}, f32[2,2,8,128]{3,2,1,0:T(8,128)S(1)}, f32[]{:T(128)}, s32[2]{0:T(128)S(1)}, f32[16,128]{1,0:T(8,128)S(1)}, /*index=5*/f32[40,2,16,1...) while((s32[]{:T(128)}, f32[2,2,8,128]{3,2,1,0:T(8,128)S(1)}, ...), condition=%wide.region_21.22_spmd.clone, body=%wide.region_20.21_spmd.clone.sunk | while | flops 200904704 | bytes 3322067 | solution.py:204
  113.6 1.7 %fusion.114 = f32[1024,80]{0,1:T(8,128)S(1)} fusion(bf16[1152,80]{0,1:T(8,128)(2,1)S(1)} %convert_element_type.130, f32[1152]{0:T(1024)S(1)} %sub.217, f32[1024]{0:T(1024)S(1)} %get-tuple-element.322, f32[1152]{0:T(1024)S(1)} %sub.218, f32[1024]{0:T(1024)S(1)} %get-tuple-element.323), kind=kOutput, calls=%fused_computation.5.clone.1 | convolution fusion | flops 200540160 | bytes 529408 | tf_op jit(solution)/shard_map/while/body/eval_jaxpr/dot_general | solution.py:192
  117.5 1.7 %fusion.114 = f32[1024,80]{0,1:T(8,128)S(1)} fusion(bf16[1152,80]{0,1:T(8,128)(2,1)S(1)} %convert_element_type.130, f32[1152]{0:T(1024)S(1)} %sub.217, f32[1024]{0:T(1024)S(1)} %get-tuple-element.322, f32[1152]{0:T(1024)S(1)} %sub.218, f32[1024]{0:T(1024)S(1)} %get-tuple-element.323), kind=kOutput, calls=%fused_computation.5.clone.1 | convolution fusion | flops 200540160 | bytes 529408 | tf_op jit(solution)/shard_map/while/body/eval_jaxpr/dot_general | solution.py:192
  (148 shorter events, 27.2 us)
Async XLA Ops:
  7.2 79.6 %copy-start = (f32[3,3,32,32]{3,2,1,0:T(8,128)S(1)}, f32[3,3,32,32]{3,2,1,0:T(8,128)}, u32[]{:S(2)}) copy-start(f32[3,3,32,32]{3,2,1,0:T(8,128)} %param.26) | copy-start | bytes 110596
  7.2 60.7 %all-reduce.4.cloned.1.call-start = ((), (), s32[]{:S(2)}) async-start(), calls=%async_computation | async-start | bytes 1114112 | tf_op jit(solution)/shard_map/psum | solution.py:125
  9.3 7.8 %copy-start.4 = (s32[1,1,128]{2,1,0:T(1,128)S(1)}, s32[1,1,128]{2,1,0:T(1,128)}, u32[]{:S(2)}) copy-start(s32[1,1,128]{2,1,0:T(1,128)} %param.21) | copy-start | bytes 1540
  9.3 7.8 %copy-start.5 = (s32[1,1,128]{2,1,0:T(1,128)S(1)}, s32[1,1,128]{2,1,0:T(1,128)}, u32[]{:S(2)}) copy-start(s32[1,1,128]{2,1,0:T(1,128)} %param.22) | copy-start | bytes 1540
  9.3 7.8 %copy-start.1 = (f32[2,16,128]{2,1,0:T(8,128)S(1)}, f32[2,16,128]{2,1,0:T(8,128)}, u32[]{:S(2)}) copy-start(f32[2,16,128]{2,1,0:T(8,128)} %param.18) | copy-start | bytes 49156
  10.0 9.8 %copy-start.9 = (f32[1,1,128]{2,1,0:T(1,128)S(1)}, f32[1,1,128]{2,1,0:T(1,128)}, u32[]{:S(2)}) copy-start(f32[1,1,128]{2,1,0:T(1,128)} %param.20) | copy-start | bytes 1540
  10.0 10.4 %collective-permute-start = (f32[40,2,4,128]{3,2,1,0:T(4,128)}, f32[40,2,4,128]{3,2,1,0:T(4,128)S(1)}, u32[]{:S(2)}, u32[]{:S(2)}) collective-permute-start(f32[40,2,4,128]{3,2,1,0:T(4,128)} %get-tuple-element.241), channel_id=1, source_target_pairs={{0,4},{4,8},{8,12},{1,5},{5,9},{9,13},{2,6},{6,10},{10,14},{3,7},{... | collective-permute-start | bytes 491528 | tf_op jit(solution)/shard_map/ppermute | solution.py:25
  15.1 7.6 %collective-permute-start.1 = (f32[40,2,4,128]{3,2,1,0:T(4,128)S(1)}, f32[40,2,4,128]{3,2,1,0:T(4,128)S(1)}, u32[]{:S(2)}, u32[]{:S(2)}) collective-permute-start(f32[40,2,4,128]{3,2,1,0:T(4,128)S(1)} %get-tuple-element.242), channel_id=1, source_target_pairs={{4,0},{8,4},{12,8},{5,1},{9,5},{13,9},{6,2},{10,6},{14,10},{7,3},{... | collective-permute-start | bytes 491528 | tf_op jit(solution)/shard_map/ppermute | solution.py:26
  23.6 5.8 %collective-permute-start.2 = (f32[40,2,24,4]{0,2,3,1:T(8,128)S(1)}, f32[40,2,24,4]{0,2,3,1:T(8,128)S(1)}, u32[]{:S(2)}, u32[]{:S(2)}) collective-permute-start(f32[40,2,24,4]{0,2,3,1:T(8,128)S(1)} %copy.219), channel_id=1, source_target_pairs={{0,2},{1,3},{4,6},{5,7},{8,10},{9,11},{12,14},{13,15},{16,18},{17,... | collective-permute-start | bytes 92168 | tf_op jit(solution)/shard_map/ppermute | solution.py:25
  27.5 6.5 %collective-permute-start.3 = (f32[40,2,24,4]{0,2,3,1:T(8,128)S(1)}, f32[40,2,24,4]{0,2,3,1:T(8,128)S(1)}, u32[]{:S(2)}, u32[]{:S(2)}) collective-permute-start(f32[40,2,24,4]{0,2,3,1:T(8,128)S(1)} %copy.220), channel_id=1, source_target_pairs={{2,0},{3,1},{6,4},{7,5},{10,8},{11,9},{14,12},{15,13},{18,16},{19,... | collective-permute-start | bytes 92168 | tf_op jit(solution)/shard_map/ppermute | solution.py:26
  39.5 5.8 %copy-start.6 = (f32[1,1,128]{2,1,0:T(1,128)S(1)}, f32[1,1,128]{2,1,0:T(1,128)}, u32[]{:S(2)}) copy-start(f32[1,1,128]{2,1,0:T(1,128)} %param.19) | copy-start | bytes 1540
  40.5 0.8 copy-start.2
  70.8 1.7 %copy-start.10 = (f32[3,3,8,32]{3,2,1,0:T(8,128)S(1)}, f32[3,3,8,32]{3,2,1,0:T(8,128)}, u32[]{:S(2)}) copy-start(f32[3,3,8,32]{3,2,1,0:T(8,128)} %param.24) | copy-start | bytes 27652
  70.8 1.7 %copy-start.11 = (f32[32]{0:T(128)S(1)}, f32[32]{0:T(128)}, u32[]{:S(2)}) copy-start(f32[32]{0:T(128)} %param.25) | copy-start | bytes 388
  70.8 1.7 %copy-start.13 = (pred[8,17]{0,1:T(8,128)(4,1)S(1)}, pred[8,17]{0,1:T(8,128)(4,1)}, u32[]{:S(2)}) copy-start(pred[8,17]{0,1:T(8,128)(4,1)} %constant.231) | copy-start | bytes 412
  86.6 0.7 copy-start.12
  92.4 0.7 copy-start.7
  92.4 0.7 copy-start.8
  95.7 2.8 %collective-permute-start.4 = (f32[1,1,44,128]{3,2,1,0:T(8,128)S(1)}, f32[1,1,44,128]{3,2,1,0:T(8,128)S(1)}, u32[]{:S(2)}, u32[]{:S(2)}) collective-permute-start(f32[1,1,44,128]{3,2,1,0:T(8,128)S(1)} %bitcast.252), channel_id=1, source_target_pairs={{0,4},{4,8},{8,12},{1,5},{5,9},{9,13},{2,6},{6,10},{10,14},{3,7},{... | collective-permute-start | bytes 67592 | tf_op jit(solution)/shard_map/ppermute | solution.py:25
  97.0 5.7 %collective-permute-start.5 = (f32[1,1,44,128]{3,2,1,0:T(8,128)S(1)}, f32[1,1,44,128]{3,2,1,0:T(8,128)S(1)}, u32[]{:S(2)}, u32[]{:S(2)}) collective-permute-start(f32[1,1,44,128]{3,2,1,0:T(8,128)S(1)} %bitcast.253), channel_id=1, source_target_pairs={{4,0},{8,4},{12,8},{5,1},{9,5},{13,9},{6,2},{10,6},{14,10},{7,3},{... | collective-permute-start | bytes 67592 | tf_op jit(solution)/shard_map/ppermute | solution.py:26
  102.7 4.4 %collective-permute-start.6 = (f32[3,1,44,128]{3,2,1,0:T(8,128)S(1)}, f32[3,1,44,128]{3,2,1,0:T(8,128)S(1)}, u32[]{:S(2)}, u32[]{:S(2)}) collective-permute-start(f32[3,1,44,128]{3,2,1,0:T(8,128)S(1)} %pad_maximum_fusion.4), channel_id=1, source_target_pairs={{0,2},{1,3},{4,6},{5,7},{8,10},{9,11},{12,14},{13,15},{16,18},{17,... | collective-permute-start | bytes 202760 | tf_op jit(solution)/shard_map/ppermute | solution.py:25
  105.1 6.2 %collective-permute-start.7 = (f32[3,1,44,128]{3,2,1,0:T(8,128)S(1)}, f32[3,1,44,128]{3,2,1,0:T(8,128)S(1)}, u32[]{:S(2)}, u32[]{:S(2)}) collective-permute-start(f32[3,1,44,128]{3,2,1,0:T(8,128)S(1)} %pad_maximum_fusion.4), channel_id=1, source_target_pairs={{2,0},{3,1},{6,4},{7,5},{10,8},{11,9},{14,12},{15,13},{18,16},{19,... | collective-permute-start | bytes 202760 | tf_op jit(solution)/shard_map/ppermute | solution.py:26
  119.4 0.6 copy-start.3
Sparse Core Ops, SparseCore 0:
  41.4 18.0 all-reduce.3
where the time goes:
time: 127 us
  blocking collectives  23.1 us (18%)
  local copies, waits for them, and re-layouts  22.2 us (17%)
  between operations  18.5 us (15%)
  starting transfers between devices  17.3 us (14%)
  matrix products  16.2 us (13%)
  waiting for transfers between devices  15.6 us (12%)
  other arithmetic  12.3 us (10%)
  loops' own time  1.56 us (1%)
    psum x1, blocking collectives, per_device(): lax.psum((jnp.sum(jnp.where(usable, misfit * misfit, 0.0)), jnp.sum(jnp.w...  19.3 us
    ppermute x4, waiting for transfers between devices, extended(): after = lax.ppermute(initial, axis, down)  14.7 us
    ppermute x4, starting transfers between devices, extended(): before = lax.ppermute(last, axis, up)  12.1 us
    conv_general_dilated x2, matrix products, valid_conv(): lax.conv_general_dilated(inputs[None], kernel, (1, 1), 'VALID', dimension...  11.5 us
    unnamed x43, local copies, waits for them, and re-layouts  5.89 us
    ppermute x4, starting transfers between devices, extended(): after = lax.ppermute(initial, axis, down)  5.16 us
    psum x1, blocking collectives, per_device(): lax.psum((squares, products, own_anom, own_mean), 'lev')  3.73 us
    max x2, local copies, waits for them, and re-layouts, per_device(): jax.nn.relu(valid_conv(features, conv1_weight) + conv1_bias[:, None, None])  3.61 us
  transfers between devices with their start and end apart: 9, of which 6 were waited for; matrix products, arithmetic and copies ran while one was open for 4% of the time, Pallas kernels for 0%

commit v1 on v0

v1 whole, which is shorter than its diff:
```python
import functools

import jax
import jax.numpy as jnp
from jax import lax
from jax.experimental import pallas as pl
from jax.experimental.pallas import tpu as pltpu
from jax.sharding import PartitionSpec as P

STEP = 2
VCUT = 6
CUT = 6
RIM = 4
EPS = 1e-06
MOVES = ((-1, -1), (-1, 0), (-1, 1), (0, -1), (0, 1), (1, -1), (1, 0), (1, 1))
MESH = pl.DeviceIdType.MESH
F32 = jnp.float32
BF16 = jnp.bfloat16


def split_two(x):
    high = x.astype(BF16)
    return high, (x - high.astype(F32)).astype(BF16)


def split_three(x):
    high = x.astype(BF16)
    rest = x - high.astype(F32)
    middle = rest.astype(BF16)
    return high, middle, (rest - middle.astype(F32)).astype(BF16)


def dot(a, b, ca=1, cb=0):
    return lax.dot_general(a, b, (((ca,), (cb,)), ((), ())), preferred_element_type=F32)


def kernel(
    gxn,
    gyn,
    members,
    a_in,
    back_ref,
    obs_ref,
    wts_ref,
    inc_ref,
    taper_ref,
    main,
    ext,
    ecol,
    erecv,
    opart,
    opeer,
    opack,
    orecv,
    sums,
    speer,
    wown,
    wrecv,
    stat,
    srecv,
    feat,
    hid,
    near,
    coef,
    halo_send,
    halo_recv,
    obs_send,
    obs_recv,
    wt_send,
    wt_recv,
    st_send,
    st_recv,
    lev_send,
    lev_recv,
):
    rows, both, cols = a_in.shape
    total_levels = 2 * 2
    g = lax.axis_index("groups")
    gx = lax.axis_index("gx")
    gy = lax.axis_index("gy")
    lev = lax.axis_index("lev")
    peer = (g, gx, gy, 1 - lev)
    first = (lev * 2).astype(F32)

    barrier = pltpu.get_barrier_semaphore()
    pl.semaphore_signal(barrier, inc=1, device_id=peer, device_id_type=MESH)
    others = [(i, j) for i in range(gxn) for j in range(gyn) if (i, j) != (0, 0)]
    for i, j in others:
        pl.semaphore_signal(
            barrier,
            inc=1,
            device_id=(g, lax.rem(gx + i, gxn), lax.rem(gy + j, gyn), lev),
            device_id_type=MESH,
        )

    def exists(dr, dc):
        nx, ny = gx + dr, gy + dc
        return (nx >= 0) & (nx < gxn) & (ny >= 0) & (ny < gyn)

    src_rows = {1: (rows - RIM, RIM), 0: (0, rows), -1: (0, RIM)}
    dst_rows = {1: (0, RIM), 0: (RIM, rows), -1: (RIM + rows, RIM)}

    def halo_copy(d):
        dr, dc = MOVES[d]
        s0, n = src_rows[dr]
        t0, _ = dst_rows[dr]
        if dc == 0:
            src = main.at[pl.ds(RIM + s0, n)]
            dst = main.at[pl.ds(t0, n)]
        else:
            src = ecol.at[pl.ds(s0, n)]
            dst = erecv.at[pl.ds(t0, n), pl.ds(0 if dc == 1 else 8, 8)]
        return pltpu.make_async_remote_copy(
            src_ref=src,
            dst_ref=dst,
            send_sem=halo_send.at[d],
            recv_sem=halo_recv.at[d],
            device_id=(g, gx + dr, gy + dc, lev),
            device_id_type=MESH,
        )

    def near_copy(d, src, dst, send, recv):
        dr, dc = MOVES[d]
        return pltpu.make_async_remote_copy(
            src_ref=src,
            dst_ref=dst.at[d],
            send_sem=send.at[d],
            recv_sem=recv.at[d],
            device_id=(g, gx + dr, gy + dc, lev),
            device_id_type=MESH,
        )

    def start_all(copy):
        for d, (dr, dc) in enumerate(MOVES):
            pl.when(exists(dr, dc))(lambda d=d: copy(d).start())

    def recv_all(copy):
        for d, (dr, dc) in enumerate(MOVES):
            pl.when(exists(-dr, -dc))(lambda d=d: copy(d).wait_recv())

    def sent_all(copy):
        for d, (dr, dc) in enumerate(MOVES):
            pl.when(exists(dr, dc))(lambda d=d: copy(d).wait_send())

    obs_copy = lambda d: near_copy(d, opack, orecv, obs_send, obs_recv)
    wt_copy = lambda d: near_copy(d, wown, wrecv, wt_send, wt_recv)

    def lev_copy(k, src, dst):
        return pltpu.make_async_remote_copy(
            src_ref=src,
            dst_ref=dst,
            send_sem=lev_send.at[k],
            recv_sem=lev_recv.at[k],
            device_id=peer,
            device_id_type=MESH,
        )

    c8 = lax.broadcasted_iota(jnp.int32, (8, cols), 0)
    j8 = lax.broadcasted_iota(jnp.int32, (8, cols), 1)
    pick = (j8 == jnp.where(c8 < RIM, c8, cols - 8 + c8)).astype(F32).astype(BF16)
    ecol[...] = jnp.zeros(ecol.shape, F32)

    obs = obs_ref[...]
    level, row_o, col_o, usable = obs[2:3], obs[3:4], obs[4:5], obs[5:6]
    y_sub = lax.broadcasted_iota(jnp.int32, (cols, 128), 0).astype(F32)
    onehot = (y_sub == col_o).astype(F32).astype(BF16)

    acc = jnp.zeros((both, 128), F32)
    for r in range(rows):
        slab = a_in[r]
        main[RIM + r] = slab
        parts = split_three(slab)
        ecol[r, :, 0:both] = sum(dot(pick, p, 1, 1) for p in parts)
        got = sum(dot(p, onehot) for p in parts)
        acc = acc + jnp.where(row_o == float(r), got, 0.0)
    mean = sum(dot(p, onehot) for p in split_three(back_ref[...].reshape(2 * rows, cols)))
    place = lax.broadcasted_iota(jnp.int32, (2 * rows, 128), 0).astype(F32)
    wanted = (level - first) * rows + row_o
    mean = jnp.sum(jnp.where(place == wanted, mean, 0.0), axis=0, keepdims=True)
    mine = jnp.where(level == first, acc[:members], 0.0) + jnp.where(
        level == first + 1.0, acc[members:], 0.0
    )
    opart[0:members] = mine
    opart[members : members + 8] = jnp.broadcast_to(mean, (8, 128))

    for d, (dr, dc) in enumerate(MOVES):
        t0, n = dst_rows[dr]

        @pl.when(jnp.logical_not(exists(-dr, -dc)))
        def _(d=d, dr=dr, dc=dc, t0=t0, n=n):
            if dc == 0:
                main[t0 : t0 + n] = jnp.zeros((n, both, cols), F32)
            else:
                c0 = 0 if dc == 1 else 8
                erecv[t0 : t0 + n, c0 : c0 + 8] = jnp.zeros((n, 8, 128), F32)
            orecv[d] = jnp.zeros(orecv.shape[1:], F32)
            wrecv[d] = jnp.zeros(wrecv.shape[1:], F32)

    pl.semaphore_wait(barrier, gxn * gyn)
    start_all(halo_copy)
    lev_obs = lev_copy(0, opart, opeer)
    lev_obs.start()
    lev_obs.wait_recv()
    full = opart[...] + opeer[...]
    anom_o = full[0:members]
    misfit = obs[0:1] - full[members : members + 1]
    error = obs[1:2]
    spread = jnp.sum(anom_o * anom_o, axis=0, keepdims=True) / (members - 1)
    on = usable > 0.5
    opack[0:members] = anom_o
    opack[members : members + 8] = obs
    start_all(obs_copy)
    stat[...] = jnp.concatenate(
        [
            jnp.where(on, misfit * misfit, 0.0),
            jnp.where(on, spread, 0.0),
            jnp.where(on, error, 0.0),
            jnp.zeros((5, 128), F32),
        ],
        0,
    )

    def stat_copy(k):
        i, j = others[k]
        return pltpu.make_async_remote_copy(
            src_ref=stat,
            dst_ref=srecv.at[k],
            send_sem=st_send.at[k],
            recv_sem=st_recv.at[k],
            device_id=(g, lax.rem(gx + i, gxn), lax.rem(gy + j, gyn), lev),
            device_id_type=MESH,
        )

    for k in range(len(others)):
        stat_copy(k).start()

    recv_all(halo_copy)

    c16 = lax.broadcasted_iota(jnp.int32, (16, cols), 0)
    j16 = lax.broadcasted_iota(jnp.int32, (16, cols), 1)
    put = (
        ((j16 < RIM) & (c16 == j16 + 8)) | ((j16 >= cols - RIM) & (c16 == j16 - (cols - 8)))
    ).astype(F32).astype(BF16)
    wide = 2 * cols
    for e in range(rows + 2 * RIM):
        ext[e, :, 0:cols] = main[e]
        spread_out = sum(dot(p, put, 0, 0) for p in split_three(erecv[e]))
        ext[e, :, cols:wide] = spread_out[0:both]

    extent = rows + 2 * RIM

    def row_sums(e, carry):
        here = ext[e]
        below = ext[jnp.minimum(e + STEP, extent - 1)]
        terms = (
            here * here,
            here * pltpu.roll(below, STEP, 1),
            here * below,
            here * pltpu.roll(below, wide - STEP, 1),
            here * pltpu.roll(here, wide - STEP, 1),
        )
        for k, term in enumerate(terms):
            sums[k, pl.ds(e, 1)] = jnp.sum(term, axis=0, keepdims=True)
        return carry

    lax.fori_loop(0, extent, row_sums, 0)
    lev_sum = lev_copy(1, sums, speer)
    lev_sum.start()
    lev_sum.wait_recv()

    weight_total = float(members * total_levels)
    sq = (sums[0] + speer[0]) / weight_total + EPS
    q0, q1, q2, q3 = [(sums[k] + speer[k]) / weight_total for k in range(1, 5)]
    top = extent - STEP
    s_here, s_below = sq[0:top], sq[STEP:extent]
    g0 = q0[0:top] / jnp.sqrt(s_here * pltpu.roll(s_below, STEP, 1))
    g1 = q1[0:top] / jnp.sqrt(s_here * s_below)
    g2 = q2[0:top] / jnp.sqrt(s_here * pltpu.roll(s_below, wide - STEP, 1))
    g3 = q3[0:top] / jnp.sqrt(s_here * pltpu.roll(s_here, wide - STEP, 1))
    up, dn = slice(0, top - STEP), slice(STEP, top)
    channels = (
        pltpu.roll(g2[up], STEP, 1),
        g1[up],
        pltpu.roll(g0[up], wide - STEP, 1),
        pltpu.roll(g3[dn], STEP, 1),
        g3[dn],
        g0[dn],
        g1[dn],
        g2[dn],
    )
    for k, channel in enumerate(channels):
        feat[:, k, :] = channel

    wts = wts_ref[...]
    w2h, w2l = split_two(wts[:, 0:96])
    w1h, w1l = split_two(wts[:, 96:120])
    w1s, w2s = jnp.concatenate([w1h, w1l], 0), jnp.concatenate([w2h, w2l], 0)
    b1, b2, hw = wts[0:32, 120:121], wts[0:32, 121:122], wts[0:32, 122:123]
    hb = wts[0:1, 123:124]
    lane = lax.broadcasted_iota(jnp.int32, (1, wide), 1)
    col_at = jnp.where(lane < cols + cols // 2, lane, lane - wide) + gy * cols
    col_in = (col_at >= 0) & (col_at < gyn * cols)

    def conv_row(x, wh, ws):
        patch = jnp.concatenate([pltpu.roll(x, 1, 1), x, pltpu.roll(x, wide - 1, 1)], 0)
        high, low = split_two(patch)
        z = dot(ws, high)
        return z[0:96] + z[96:192] + dot(wh, low)

    z1 = [conv_row(feat[i], w1h, w1s) for i in range(3)]
    z2 = []
    tapers = []
    for i in range(rows + 2):
        h = z1[0][0:32] + z1[1][32:64] + z1[2][64:96]
        if i + 3 < rows + 4:
            z1 = [z1[1], z1[2], conv_row(feat[i + 3], w1h, w1s)]
        row_at = gx * rows + (i - 1)
        keep = col_in & (row_at >= 0) & (row_at < gxn * rows)
        h = jnp.where(keep, jnp.maximum(h + b1, 0.0), 0.0)
        z2.append(conv_row(h, w2h, w2s)[:, 0:cols])
        if len(z2) == 3:
            out = z2[0][0:32] + z2[1][32:64] + z2[2][64:96]
            out = jnp.maximum(out + b2, 0.0)
            tapers.append(jnp.sum(out * hw, axis=0, keepdims=True) + hb)
            z2 = z2[1:]
    logits = jnp.concatenate(tapers, 0)
    taper = 1.0 / (1.0 + jnp.exp(-logits))
    taper_ref[...] = taper

    for k in range(len(others)):
        stat_copy(k).wait_recv()
    tot = stat[...]
    for k in range(len(others)):
        tot = tot + srecv[k]
    tot = jnp.sum(tot, axis=1, keepdims=True)
    inflation = tot[0:1] / (tot[1:2] + tot[2:3])
    gain = jnp.where(on, misfit / (inflation * spread + error), 0.0)
    at_obs = sum(dot(p, onehot) for p in split_three(taper))
    place = lax.broadcasted_iota(jnp.int32, (rows, 128), 0).astype(F32)
    at_obs = jnp.sum(jnp.where(place == row_o, at_obs, 0.0), axis=0, keepdims=True)
    weight = at_obs * gain / (members - 1)
    wown[...] = jnp.broadcast_to(weight, (8, 128))
    start_all(wt_copy)
    recv_all(obs_copy)

    tiles = [(tr, tc) for tr in (-1, 0, 1) for tc in (-1, 0, 1)]
    row_list = []
    for t, (tr, tc) in enumerate(tiles):
        pack = opack if (tr, tc) == (0, 0) else orecv.at[MOVES.index((-tr, -tc))]
        gap = y_sub - (pack[members + 4 : members + 5] + float(tc * cols))
        near[:, t * 128 : t * 128 + 128] = gap * gap / float(CUT * CUT)
        row_list.append(pack[members + 3 : members + 4] + float(tr * rows))
    row_all = jnp.concatenate(row_list, 1)
    recv_all(wt_copy)
    for t, (tr, tc) in enumerate(tiles):
        d = None if (tr, tc) == (0, 0) else MOVES.index((-tr, -tc))
        pack = opack if d is None else orecv.at[d]
        w = weight if d is None else wrecv[d, 0:1]
        anom = pack[0:members]
        for l in range(2):
            ratio = (first + float(l) - pack[members + 2 : members + 3]) / VCUT
            vert = jnp.maximum(0.0, 1.0 - ratio * ratio)
            near_coef = (vert * vert * w) * anom
            hid[l * members : (l + 1) * members, t * 128 : t * 128 + 128] = near_coef
    coef[...] = hid[...].astype(BF16)

    for r in range(rows):
        k0 = 0 if r < CUT - 1 else 3 * 128
        k1 = 9 * 128 if r > rows - CUT else 6 * 128
        gap = float(r) - row_all[:, k0:k1]
        base = 1.0 - gap * gap / float(CUT * CUT)
        m = jnp.maximum(0.0, base - near[:, k0:k1])
        local = (m * m).astype(BF16)
        w = dot(coef[:, k0:k1], local, 1, 1)
        prod = main[RIM + r] * w
        scale = inflation * taper[r : r + 1]
        for l in range(2):
            part = jnp.sum(prod[l * members : (l + 1) * members], axis=0, keepdims=True)
            inc_ref[l, r : r + 1] = scale * part

    sent_all(halo_copy)
    sent_all(obs_copy)
    sent_all(wt_copy)
    for k in range(len(others)):
        stat_copy(k).wait_send()
    lev_obs.wait_send()
    lev_sum.wait_send()


def per_device(
    anomaly_codes,
    block_scales,
    background,
    obs_values,
    obs_error,
    obs_cell,
    obs_level,
    obs_count,
    conv1_weight,
    conv1_bias,
    conv2_weight,
    conv2_bias,
    head_weight,
    head_bias,
):
    members, levs, rows, cols = anomaly_codes.shape
    gxn, gyn = lax.axis_size("gx"), lax.axis_size("gy")
    both = members * levs
    a = (anomaly_codes.astype(F32) * block_scales).transpose(2, 1, 0, 3).reshape(rows, both, cols)
    cell = obs_cell[0]
    obs = jnp.concatenate(
        [
            obs_values[0],
            obs_error[0],
            obs_level[0].astype(F32),
            (cell // cols).astype(F32),
            (cell % cols).astype(F32),
            (jnp.arange(128)[None] < obs_count).astype(F32),
            jnp.zeros((2, 128), F32),
        ],
        0,
    )
    w2 = conv2_weight.transpose(0, 3, 1, 2).reshape(96, 96)
    w1 = conv1_weight.transpose(0, 3, 1, 2).reshape(96, 24)
    col = lambda v: jnp.tile(v, 3)[:, None]
    wts = jnp.concatenate(
        [
            w2,
            w1,
            col(conv1_bias),
            col(conv2_bias),
            col(head_weight),
            jnp.broadcast_to(head_bias[None], (96, 1)),
            jnp.zeros((96, 4), F32),
        ],
        1,
    )
    vm = lambda *s, dtype=F32: pltpu.VMEM(s, dtype)
    sem = lambda n: pltpu.SemaphoreType.DMA((n,))
    extent = rows + 2 * RIM
    tiles = gxn * gyn - 1
    return pl.pallas_call(
        functools.partial(kernel, gxn, gyn, members),
        out_shape=(
            jax.ShapeDtypeStruct((levs, rows, cols), F32),
            jax.ShapeDtypeStruct((rows, cols), F32),
        ),
        in_specs=[pl.BlockSpec(memory_space=pltpu.VMEM)] * 4,
        out_specs=[pl.BlockSpec(memory_space=pltpu.VMEM)] * 2,
        scratch_shapes=[
            vm(extent, both, cols),
            vm(extent, both, 2 * cols),
            vm(rows, 8, 128),
            vm(extent, 16, 128),
            vm(members + 8, 128),
            vm(members + 8, 128),
            vm(members + 8, 128),
            vm(8, members + 8, 128),
            vm(5, extent, 2 * cols),
            vm(5, extent, 2 * cols),
            vm(8, 128),
            vm(8, 8, 128),
            vm(8, 128),
            vm(tiles, 8, 128),
            vm(rows + 4, 8, 2 * cols),
            vm(both, 9 * 128),
            vm(cols, 9 * 128),
            vm(both, 9 * 128, dtype=BF16),
            sem(8),
            sem(8),
            sem(8),
            sem(8),
            sem(8),
            sem(8),
            sem(tiles),
            sem(tiles),
            sem(2),
            sem(2),
        ],
        compiler_params=pltpu.CompilerParams(
            collective_id=0, has_side_effects=True, vmem_limit_bytes=40 * 1024 * 1024
        ),
    )(a, background, obs, wts)


def solution(mesh):
    in_specs = (
        P(None, "lev", ("groups", "gx"), "gy"),
        P(None, "lev", ("groups", "gx"), "gy"),
        P("lev", ("groups", "gx"), "gy"),
        P(("groups", "gx"), "gy", None),
        P(("groups", "gx"), "gy", None),
        P(("groups", "gx"), "gy", None),
        P(("groups", "gx"), "gy", None),
        P(("groups", "gx"), "gy"),
        P(),
        P(),
        P(),
        P(),
        P(),
        P(),
    )
    out_specs = (P("lev", ("groups", "gx"), "gy"), P(("groups", "gx"), "gy"))
    return jax.shard_map(
        per_device, mesh=mesh, in_specs=in_specs, out_specs=out_specs, check_vma=False
    )
```

time: 127 us -> 36.3 us (0.29)
  Pallas kernels: 0 us -> 24.5 us
  blocking collectives: 23.1 us -> 0 us
  starting transfers between devices: 17.3 us -> 0 us
  between operations: 18.5 us -> 2.08 us
  matrix products: 16.2 us -> 0 us
  waiting for transfers between devices: 15.6 us -> 0 us
  local copies, waits for them, and re-layouts: 22.2 us -> 8.14 us
  other arithmetic: 12.3 us -> 1.22 us
  loops' own time: 1.56 us -> 0 us
    pallas_call x0 -> x1, Pallas kernels: none -> 24.5 us  [per_device(): pl.pallas_call(functools.partial(kernel, gxn, gyn, members), out_shape=(j...]
    psum x2 -> x0, blocking collectives: 23.1 us -> none  [the longest x1 19.3 us: per_device(): lax.psum((jnp.sum(jnp.where(usable, misfit * misfit, 0.0)), jnp.sum(jnp.w...]
    ppermute x8 -> x0, starting transfers between devices: 17.3 us -> none  [the longest x4 12.1 us: extended(): before = lax.ppermute(last, axis, up)]
    ppermute x8 -> x0, waiting for transfers between devices: 15.6 us -> none  [the longest x4 14.7 us: extended(): after = lax.ppermute(initial, axis, down)]
    conv_general_dilated x2 -> x0, matrix products: 11.5 us -> none  [valid_conv(): lax.conv_general_dilated(inputs[None], kernel, (1, 1), 'VALID', dimension...]
    reduce_sum x5 -> x0, other arithmetic: 5.15 us -> none  [the longest x1 2.62 us: local_sums(): product_list.append(jnp.sum(centre * shifted, axis=(0, 1)) / weight_total)]
    dot_general x3 -> x0, matrix products: 4.75 us -> none  [the longest x2 3.47 us: update(): jnp.dot(localization, coeff_matrix, preferred_element_type=jnp.float32)]
    max x2 -> x0, local copies, waits for them, and re-layouts: 3.61 us -> none  [per_device(): jax.nn.relu(valid_conv(features, conv1_weight) + conv1_bias[:, None, None])]
  transfers between devices with their start and end apart: 9 -> 0, of which waited for: 6 -> 0; matrix products, arithmetic and copies ran while one was open for 4% -> 0% of each run, Pallas kernels for 0% -> 0%
where the time goes in v1:
time: 36.3 us; the launch traced here: 35.9 us
  Pallas kernels  24.5 us (67%)
  local copies, waits for them, and re-layouts  8.14 us (22%)
  between operations  2.08 us (6%)
  other arithmetic  1.22 us (3%)
    pallas_call x1, Pallas kernels, per_device(): pl.pallas_call(functools.partial(kernel, gxn, gyn, members), out_shape=(j...  24.5 us
    unnamed x22, local copies, waits for them, and re-layouts  6.01 us
    transpose x1, other arithmetic, per_device(): (anomaly_codes.astype(F32) * block_scales).transpose(2, 1, 0, 3)  1.2 us
    mul x1, local copies, waits for them, and re-layouts, per_device(): anomaly_codes.astype(F32) * block_scales  0.8 us

profile of v1, /device:TPU:0, one launch (start us, length us, event | category | flops | bytes accessed | tf_op | source)
XLA Modules:
  0.0 35.9 jit_solution(14360513955138729959)
XLA Ops:
  0.6 0.8 %copy.23 = f32[40,2,16]{2,1,0:T(2,128)S(1)} copy(f32[40,2,16]{0,2,1:T(8,128)} %bitcast.36) | data formatting | bytes 10240 | tf_op jit(solution)/shard_map/mul | solution.py:409
  1.4 1.2 %multiply_bitcast_fusion = f32[16,2,40,128]{3,0,1,2:T(8,128)S(1)} fusion(bf16[40,2,16,128]{3,2,1,0:T(8,128)(2,1)} %param.14, f32[40,2,16]{2,1,0:T(2,128)S(1)} %copy.23), kind=kLoop, calls=%fused_computation | loop fusion | flops 327680 | bytes 988160 | tf_op jit(solution)/shard_map/transpose | solution.py:409
  2.7 0.4 %copy.24 = f32[16,2,40,128]{3,2,1,0:T(8,128)S(1)} copy(f32[16,2,40,128]{3,0,1,2:T(8,128)S(1)} %multiply_bitcast_fusion) | data formatting | bytes 1310720 | tf_op jit(solution)/shard_map/transpose | solution.py:409
  3.0 0.0 copy-start.8
  3.1 0.6 %copy-done.8 = s32[1,1,128]{2,1,0:T(1,128)S(1)} copy-done((s32[1,1,128]{2,1,0:T(1,128)S(1)}, s32[1,1,128]{2,1,0:T(1,128)}, u32[]{:S(2)}) %copy-start.8) | copy-done | bytes 536
  3.7 0.7 %copy-done.9 = s32[1,1,128]{2,1,0:T(1,128)S(1)} copy-done((s32[1,1,128]{2,1,0:T(1,128)S(1)}, s32[1,1,128]{2,1,0:T(1,128)}, u32[]{:S(2)}) %copy-start.9) | copy-done | bytes 536
  5.1 0.6 %copy-done.3 = f32[1,1,128]{2,1,0:T(1,128)S(1)} copy-done((f32[1,1,128]{2,1,0:T(1,128)S(1)}, f32[1,1,128]{2,1,0:T(1,128)}, u32[]{:S(2)}) %copy-start.3) | copy-done | bytes 536
  5.7 0.0 copy-done.4
  5.7 0.1 copy.25
  5.9 0.1 reshape.195
  6.0 0.6 %copy-done.2 = f32[3,3,8,32]{3,2,1,0:T(8,128)S(1)} copy-done((f32[3,3,8,32]{3,2,1,0:T(8,128)S(1)}, f32[3,3,8,32]{3,2,1,0:T(8,128)}, u32[]{:S(2)}) %copy-start.2) | copy-done | bytes 9240
  6.7 0.1 reshape.196
  6.7 0.1 copy.27
  6.8 0.6 %copy-done.5 = f32[32]{0:T(128)S(1)} copy-done((f32[32]{0:T(128)S(1)}, f32[32]{0:T(128)}, u32[]{:S(2)}) %copy-start.5) | copy-done | bytes 152
  7.4 0.1 broadcast_in_dim_tile.12
  7.5 0.5 %copy-done.6 = f32[32]{0:T(128)S(1)} copy-done((f32[32]{0:T(128)S(1)}, f32[32]{0:T(128)}, u32[]{:S(2)}) %copy-start.6) | copy-done | bytes 152
  8.1 0.1 broadcast_in_dim_tile.13
  8.2 0.5 %copy-done.7 = f32[32]{0:T(128)S(1)} copy-done((f32[32]{0:T(128)S(1)}, f32[32]{0:T(128)}, u32[]{:S(2)}) %copy-start.7) | copy-done | bytes 152
  8.7 0.1 broadcast_in_dim_tile.14
  9.5 0.1 concatenate.7.wts_ref
  9.7 0.6 %copy-done = f32[2,16,128]{2,1,0:T(8,128)S(1)} copy-done((f32[2,16,128]{2,1,0:T(8,128)S(1)}, f32[2,16,128]{2,1,0:T(8,128)}, u32[]{:S(2)}) %copy-start) | copy-done | bytes 16408
  10.2 24.5 %shard_map.149 = (f32[2,16,128]{2,1,0:T(8,128)S(1)}, f32[16,128]{1,0:T(8,128)S(1)}) custom-call(f32[16,80,128]{2,1,0:T(8,128)S(1)} %bitcast.33, f32[2,16,128]{2,1,0:T(8,128)S(1)} %copy-done, f32[8,128]{1,0:T(8,128)S(1)} %concatenate.6.obs_ref, f32[96,128]{1,0:T(8,128)S(1)} %concatenate.7.wts_ref), custom_call_target="tpu_custom_call" | custom-call | tf_op jit(solution)/shard_map/pallas_call | solution.py:442
  34.7 0.6 %copy.35 = f32[2,16,128]{2,1,0:T(8,128)} copy(f32[2,16,128]{2,1,0:T(8,128)S(1)} %get-tuple-element.6) | data formatting | bytes 32768
  35.3 0.6 %copy.36 = f32[16,128]{1,0:T(8,128)} copy(f32[16,128]{1,0:T(8,128)S(1)} %get-tuple-element.7) | data formatting | bytes 16384
  (21 shorter events, 0.1 us)
Async XLA Ops:
  2.6 3.1 %copy-start.1 = (f32[3,3,32,32]{3,2,1,0:T(8,128)S(1)}, f32[3,3,32,32]{3,2,1,0:T(8,128)}, u32[]{:S(2)}) copy-start(f32[3,3,32,32]{3,2,1,0:T(8,128)} %param.24) | copy-start | bytes 110596
  3.0 0.7 %copy-start.8 = (s32[1,1,128]{2,1,0:T(1,128)S(1)}, s32[1,1,128]{2,1,0:T(1,128)}, u32[]{:S(2)}) copy-start(s32[1,1,128]{2,1,0:T(1,128)} %param.20) | copy-start | bytes 1540
  3.7 0.7 %copy-start.9 = (s32[1,1,128]{2,1,0:T(1,128)S(1)}, s32[1,1,128]{2,1,0:T(1,128)}, u32[]{:S(2)}) copy-start(s32[1,1,128]{2,1,0:T(1,128)} %param.19) | copy-start | bytes 1540
  5.0 0.7 %copy-start.3 = (f32[1,1,128]{2,1,0:T(1,128)S(1)}, f32[1,1,128]{2,1,0:T(1,128)}, u32[]{:S(2)}) copy-start(f32[1,1,128]{2,1,0:T(1,128)} %param.17) | copy-start | bytes 1540
  5.0 0.7 %copy-start.4 = (f32[1,1,128]{2,1,0:T(1,128)S(1)}, f32[1,1,128]{2,1,0:T(1,128)}, u32[]{:S(2)}) copy-start(f32[1,1,128]{2,1,0:T(1,128)} %param.18) | copy-start | bytes 1540
  5.9 0.8 %copy-start.2 = (f32[3,3,8,32]{3,2,1,0:T(8,128)S(1)}, f32[3,3,8,32]{3,2,1,0:T(8,128)}, u32[]{:S(2)}) copy-start(f32[3,3,8,32]{3,2,1,0:T(8,128)} %param.22) | copy-start | bytes 27652
  6.7 0.7 %copy-start.5 = (f32[32]{0:T(128)S(1)}, f32[32]{0:T(128)}, u32[]{:S(2)}) copy-start(f32[32]{0:T(128)} %param.23) | copy-start | bytes 388
  7.4 0.7 %copy-start.6 = (f32[32]{0:T(128)S(1)}, f32[32]{0:T(128)}, u32[]{:S(2)}) copy-start(f32[32]{0:T(128)} %param.25) | copy-start | bytes 388
  8.1 0.7 %copy-start.7 = (f32[32]{0:T(128)S(1)}, f32[32]{0:T(128)}, u32[]{:S(2)}) copy-start(f32[32]{0:T(128)} %param.26) | copy-start | bytes 388
  9.5 0.7 %copy-start = (f32[2,16,128]{2,1,0:T(8,128)S(1)}, f32[2,16,128]{2,1,0:T(8,128)}, u32[]{:S(2)}) copy-start(f32[2,16,128]{2,1,0:T(8,128)} %back_ref.1) | copy-start | bytes 49156

commit v2 on v1

--- a/solution.py
+++ b/solution.py
@@ -38,10 +38,20 @@
     gxn,
     gyn,
     members,
-    a_in,
+    codes_ref,
+    scale_ref,
     back_ref,
-    obs_ref,
-    wts_ref,
+    values_ref,
+    error_ref,
+    cell_ref,
+    level_ref,
+    count_ref,
+    c1_ref,
+    c2_ref,
+    b1_ref,
+    b2_ref,
+    hw_ref,
+    hb_ref,
     inc_ref,
     taper_ref,
     main,
@@ -62,6 +72,10 @@
     hid,
     near,
     coef,
+    flat,
+    scales,
+    wtile,
+    local,
     halo_send,
     halo_recv,
     obs_send,
@@ -73,7 +87,8 @@
     lev_send,
     lev_recv,
 ):
-    rows, both, cols = a_in.shape
+    _, levs, rows, cols = codes_ref.shape
+    both = members * levs
     total_levels = 2 * 2
     g = lax.axis_index("groups")
     gx = lax.axis_index("gx")
@@ -155,34 +170,20 @@
             device_id_type=MESH,
         )
 
-    c8 = lax.broadcasted_iota(jnp.int32, (8, cols), 0)
-    j8 = lax.broadcasted_iota(jnp.int32, (8, cols), 1)
-    pick = (j8 == jnp.where(c8 < RIM, c8, cols - 8 + c8)).astype(F32).astype(BF16)
-    ecol[...] = jnp.zeros(ecol.shape, F32)
-
-    obs = obs_ref[...]
-    level, row_o, col_o, usable = obs[2:3], obs[3:4], obs[4:5], obs[5:6]
-    y_sub = lax.broadcasted_iota(jnp.int32, (cols, 128), 0).astype(F32)
-    onehot = (y_sub == col_o).astype(F32).astype(BF16)
-
-    acc = jnp.zeros((both, 128), F32)
+    for l in range(levs):
+        for r in range(rows):
+            scales[l * rows + r : l * rows + r + 1, 0:members] = scale_ref[l, r]
+    flat[...] = codes_ref[...].reshape(both * rows, cols).astype(F32)
+    scale_cols = scales[...].T
+    spans = [slice(l * members, (l + 1) * members) for l in range(levs)]
+
+    def code_slab(l, r):
+        return flat[pl.ds(l * rows + r, members, stride=levs * rows)]
+
     for r in range(rows):
-        slab = a_in[r]
-        main[RIM + r] = slab
-        parts = split_three(slab)
-        ecol[r, :, 0:both] = sum(dot(pick, p, 1, 1) for p in parts)
-        got = sum(dot(p, onehot) for p in parts)
-        acc = acc + jnp.where(row_o == float(r), got, 0.0)
-    mean = sum(dot(p, onehot) for p in split_three(back_ref[...].reshape(2 * rows, cols)))
-    place = lax.broadcasted_iota(jnp.int32, (2 * rows, 128), 0).astype(F32)
-    wanted = (level - first) * rows + row_o
-    mean = jnp.sum(jnp.where(place == wanted, mean, 0.0), axis=0, keepdims=True)
-    mine = jnp.where(level == first, acc[:members], 0.0) + jnp.where(
-        level == first + 1.0, acc[members:], 0.0
-    )
-    opart[0:members] = mine
-    opart[members : members + 8] = jnp.broadcast_to(mean, (8, 128))
-
+        for l in range(levs):
+            at = l * rows + r
+            main[RIM + r, spans[l]] = code_slab(l, r) * scale_cols[0:members, at : at + 1]
     for d, (dr, dc) in enumerate(MOVES):
         t0, n = dst_rows[dr]
 
@@ -196,19 +197,69 @@
             orecv[d] = jnp.zeros(orecv.shape[1:], F32)
             wrecv[d] = jnp.zeros(wrecv.shape[1:], F32)
 
+    c8 = lax.broadcasted_iota(jnp.int32, (8, cols), 0)
+    j8 = lax.broadcasted_iota(jnp.int32, (8, cols), 1)
+    pick = (j8 == jnp.where(c8 < RIM, c8, cols - 8 + c8)).astype(F32).astype(BF16)
+    ecol[...] = jnp.zeros(ecol.shape, F32)
+    for r in range(rows):
+        ecol[r, :, 0:both] = sum(dot(pick, p, 1, 1) for p in split_two(main[RIM + r]))
+
+    cell = cell_ref[0]
+    level = level_ref[0].astype(F32)
+    row_o, col_o = (cell // cols).astype(F32), lax.rem(cell, cols).astype(F32)
+    on = lax.broadcasted_iota(jnp.int32, (1, 128), 1) < count_ref[...]
+    error = error_ref[0]
+    y_sub = lax.broadcasted_iota(jnp.int32, (cols, 128), 0).astype(F32)
+    onehot = (y_sub == col_o).astype(F32).astype(BF16)
+
     pl.semaphore_wait(barrier, gxn * gyn)
     start_all(halo_copy)
+
+    mine = jnp.zeros((members, 128), F32)
+    for r in range(rows):
+        for l in range(levs):
+            at = l * rows + r
+            got = dot(code_slab(l, r).astype(BF16), onehot) * scale_cols[0:members, at : at + 1]
+            mine = mine + jnp.where((row_o == float(r)) & (level == first + float(l)), got, 0.0)
+    mean = sum(dot(p, onehot) for p in split_three(back_ref[...].reshape(2 * rows, cols)))
+    place = lax.broadcasted_iota(jnp.int32, (2 * rows, 128), 0).astype(F32)
+    wanted = (level - first) * rows + row_o
+    mean = jnp.sum(jnp.where(place == wanted, mean, 0.0), axis=0, keepdims=True)
+    opart[0:members] = mine
+    opart[members : members + 8] = jnp.broadcast_to(mean, (8, 128))
+
     lev_obs = lev_copy(0, opart, opeer)
     lev_obs.start()
+    wtile[...] = jnp.zeros(wtile.shape, F32)
+    chans, feats = c2_ref.shape[2], c1_ref.shape[2]
+    for i in range(3):
+        for j in range(3):
+            lanes = slice(i * chans, (i + 1) * chans)
+            wtile[j * chans : (j + 1) * chans, lanes] = c2_ref[i, j]
+            wtile[96 + j * feats : 96 + (j + 1) * feats, lanes] = c1_ref[i, j]
+    wtile[120:121, 0:chans] = b1_ref[...]
+    wtile[121:122, 0:chans] = b2_ref[...]
+    wtile[122:123, 0:chans] = hw_ref[...]
+    wts = wtile[...].T
+    w2h, w2l = split_two(wts[0:96, 0:96])
+    w1h, w1l = split_two(wts[0:96, 96:120])
+    w1s, w2s = jnp.concatenate([w1h, w1l], 0), jnp.concatenate([w2h, w2l], 0)
+    b1, b2, hw = wts[0:32, 120:121], wts[0:32, 121:122], wts[0:32, 122:123]
+    hb = hb_ref[...]
+    wide = 2 * cols
+    lane = lax.broadcasted_iota(jnp.int32, (1, wide), 1)
+    col_at = jnp.where(lane < cols + cols // 2, lane, lane - wide) + gy * cols
+    col_in = (col_at >= 0) & (col_at < gyn * cols)
+
     lev_obs.wait_recv()
     full = opart[...] + opeer[...]
     anom_o = full[0:members]
-    misfit = obs[0:1] - full[members : members + 1]
-    error = obs[1:2]
+    misfit = values_ref[0] - full[members : members + 1]
     spread = jnp.sum(anom_o * anom_o, axis=0, keepdims=True) / (members - 1)
-    on = usable > 0.5
     opack[0:members] = anom_o
-    opack[members : members + 8] = obs
+    opack[members : members + 8] = jnp.concatenate(
+        [level, level, level, row_o, col_o, jnp.zeros((3, 128), F32)], 0
+    )
     start_all(obs_copy)
     stat[...] = jnp.concatenate(
         [
@@ -241,10 +292,9 @@
     put = (
         ((j16 < RIM) & (c16 == j16 + 8)) | ((j16 >= cols - RIM) & (c16 == j16 - (cols - 8)))
     ).astype(F32).astype(BF16)
-    wide = 2 * cols
     for e in range(rows + 2 * RIM):
         ext[e, :, 0:cols] = main[e]
-        spread_out = sum(dot(p, put, 0, 0) for p in split_three(erecv[e]))
+        spread_out = sum(dot(p, put, 0, 0) for p in split_two(erecv[e]))
         ext[e, :, cols:wide] = spread_out[0:both]
 
     extent = rows + 2 * RIM
@@ -291,16 +341,6 @@
     for k, channel in enumerate(channels):
         feat[:, k, :] = channel
 
-    wts = wts_ref[...]
-    w2h, w2l = split_two(wts[:, 0:96])
-    w1h, w1l = split_two(wts[:, 96:120])
-    w1s, w2s = jnp.concatenate([w1h, w1l], 0), jnp.concatenate([w2h, w2l], 0)
-    b1, b2, hw = wts[0:32, 120:121], wts[0:32, 121:122], wts[0:32, 122:123]
-    hb = wts[0:1, 123:124]
-    lane = lax.broadcasted_iota(jnp.int32, (1, wide), 1)
-    col_at = jnp.where(lane < cols + cols // 2, lane, lane - wide) + gy * cols
-    col_in = (col_at >= 0) & (col_at < gyn * cols)
-
     def conv_row(x, wh, ws):
         patch = jnp.concatenate([pltpu.roll(x, 1, 1), x, pltpu.roll(x, wide - 1, 1)], 0)
         high, low = split_two(patch)
@@ -351,6 +391,16 @@
         near[:, t * 128 : t * 128 + 128] = gap * gap / float(CUT * CUT)
         row_list.append(pack[members + 3 : members + 4] + float(tr * rows))
     row_all = jnp.concatenate(row_list, 1)
+
+    def near_span(r):
+        return (0 if r < CUT - 1 else 3 * 128), (9 * 128 if r > rows - CUT else 6 * 128)
+
+    for r in range(rows):
+        k0, k1 = near_span(r)
+        gap = float(r) - row_all[:, k0:k1]
+        base = 1.0 - gap * gap / float(CUT * CUT)
+        m = jnp.maximum(0.0, base - near[:, k0:k1])
+        local[r, :, 0 : k1 - k0] = (m * m).astype(BF16)
     recv_all(wt_copy)
     for t, (tr, tc) in enumerate(tiles):
         d = None if (tr, tc) == (0, 0) else MOVES.index((-tr, -tc))
@@ -365,13 +415,8 @@
     coef[...] = hid[...].astype(BF16)
 
     for r in range(rows):
-        k0 = 0 if r < CUT - 1 else 3 * 128
-        k1 = 9 * 128 if r > rows - CUT else 6 * 128
-        gap = float(r) - row_all[:, k0:k1]
-        base = 1.0 - gap * gap / float(CUT * CUT)
-        m = jnp.maximum(0.0, base - near[:, k0:k1])
-        local = (m * m).astype(BF16)
-        w = dot(coef[:, k0:k1], local, 1, 1)
+        k0, k1 = near_span(r)
+        w = dot(coef[:, k0:k1], local[r, :, 0 : k1 - k0], 1, 1)
         prod = main[RIM + r] * w
         scale = inflation * taper[r : r + 1]
         for l in range(2):
@@ -406,35 +451,8 @@
     members, levs, rows, cols = anomaly_codes.shape
     gxn, gyn = lax.axis_size("gx"), lax.axis_size("gy")
     both = members * levs
-    a = (anomaly_codes.astype(F32) * block_scales).transpose(2, 1, 0, 3).reshape(rows, both, cols)
-    cell = obs_cell[0]
-    obs = jnp.concatenate(
-        [
-            obs_values[0],
-            obs_error[0],
-            obs_level[0].astype(F32),
-            (cell // cols).astype(F32),
-            (cell % cols).astype(F32),
-            (jnp.arange(128)[None] < obs_count).astype(F32),
-            jnp.zeros((2, 128), F32),
-        ],
-        0,
-    )
-    w2 = conv2_weight.transpose(0, 3, 1, 2).reshape(96, 96)
-    w1 = conv1_weight.transpose(0, 3, 1, 2).reshape(96, 24)
-    col = lambda v: jnp.tile(v, 3)[:, None]
-    wts = jnp.concatenate(
-        [
-            w2,
-            w1,
-            col(conv1_bias),
-            col(conv2_bias),
-            col(head_weight),
-            jnp.broadcast_to(head_bias[None], (96, 1)),
-            jnp.zeros((96, 4), F32),
-        ],
-        1,
-    )
+    scales = block_scales.transpose(1, 2, 3, 0)
+    row = lambda v: v.reshape(1, -1)
     vm = lambda *s, dtype=F32: pltpu.VMEM(s, dtype)
     sem = lambda n: pltpu.SemaphoreType.DMA((n,))
     extent = rows + 2 * RIM
@@ -445,7 +463,7 @@
             jax.ShapeDtypeStruct((levs, rows, cols), F32),
             jax.ShapeDtypeStruct((rows, cols), F32),
         ),
-        in_specs=[pl.BlockSpec(memory_space=pltpu.VMEM)] * 4,
+        in_specs=[pl.BlockSpec(memory_space=pltpu.VMEM)] * 14,
         out_specs=[pl.BlockSpec(memory_space=pltpu.VMEM)] * 2,
         scratch_shapes=[
             vm(extent, both, cols),
@@ -466,6 +484,10 @@
             vm(both, 9 * 128),
             vm(cols, 9 * 128),
             vm(both, 9 * 128, dtype=BF16),
+            vm(both * rows, cols),
+            vm(128, 128),
+            vm(128, 128),
+            vm(rows, cols, 6 * 128, dtype=BF16),
             sem(8),
             sem(8),
             sem(8),
@@ -480,7 +502,22 @@
         compiler_params=pltpu.CompilerParams(
             collective_id=0, has_side_effects=True, vmem_limit_bytes=40 * 1024 * 1024
         ),
-    )(a, background, obs, wts)
+    )(
+        anomaly_codes,
+        scales,
+        background,
+        obs_values,
+        obs_error,
+        obs_cell,
+        obs_level,
+        obs_count,
+        conv1_weight,
+        conv2_weight,
+        row(conv1_bias),
+        row(conv2_bias),
+        row(head_weight),
+        row(head_bias),
+    )
 
 
 def solution(mesh):

time: 36.3 us -> 32.5 us (0.90)
  local copies, waits for them, and re-layouts: 8.14 us -> 5.98 us
  other arithmetic: 1.22 us -> 0 us
  Pallas kernels: 24.5 us -> 24.1 us
    transpose x1 -> x0, other arithmetic: 1.2 us -> none  [per_device(): (anomaly_codes.astype(F32) * block_scales).transpose(2, 1, 0, 3)]
    mul x1 -> x0, local copies, waits for them, and re-layouts: 0.8 us -> none  [per_device(): anomaly_codes.astype(F32) * block_scales]
    transpose x3 -> x0, local copies, waits for them, and re-layouts: 0.53 us -> none  [the longest x1 0.38 us: per_device(): (anomaly_codes.astype(F32) * block_scales).transpose(2, 1, 0, 3)]
    pallas_call x1, Pallas kernels: 24.5 us -> 24.1 us  [per_device(): pl.pallas_call(functools.partial(kernel, gxn, gyn, members), out_shape=(j...]
    unnamed x22 -> x26, local copies, waits for them, and re-layouts: 6.01 us -> 5.98 us
where the time goes in v2:
time: 32.5 us; the launch traced here: 32.1 us
  Pallas kernels  24.1 us (74%)
  local copies, waits for them, and re-layouts  5.98 us (18%)
  between operations  2 us (6%)
    pallas_call x1, Pallas kernels, per_device(): pl.pallas_call(functools.partial(kernel, gxn, gyn, members), out_shape=(j...  24.1 us
    unnamed x26, local copies, waits for them, and re-layouts  5.98 us

profile of v2, /device:TPU:0, one launch (start us, length us, event | category | flops | bytes accessed | tf_op | source)
XLA Modules:
  0.0 32.1 jit_solution(13626103250611249243)
XLA Ops:
  1.9 0.0 copy-start.8
  1.9 0.0 copy-start.9
  1.9 0.0 copy-start.10
  2.0 0.0 copy-start.11
  2.0 0.0 copy-start.5
  2.0 0.0 copy-start.6
  2.0 0.0 copy-start.7
  2.0 0.6 %copy-done.8 = s32[1,1,128]{2,1,0:T(1,128)S(1)} copy-done((s32[1,1,128]{2,1,0:T(1,128)S(1)}, s32[1,1,128]{2,1,0:T(1,128)}, u32[]{:S(2)}) %copy-start.8) | copy-done | bytes 536
  2.6 0.0 copy-done.9
  2.6 0.0 copy-done.10
  2.6 0.0 copy-done.11
  2.6 0.0 copy-done.5
  2.6 0.0 copy-done.6
  2.7 0.0 copy-done.7
  2.7 0.0 copy-start
  2.7 1.0 %copy-done = bf16[40,2,16,128]{3,2,1,0:T(8,128)(2,1)S(1)} copy-done((bf16[40,2,16,128]{3,2,1,0:T(8,128)(2,1)S(1)}, bf16[40,2,16,128]{3,2,1,0:T(8,128)(2,1)}, u32[]{:S(2)}) %copy-start) | copy-done | bytes 327704
  3.7 0.0 copy-start.1
  3.7 0.9 %copy-done.1 = f32[3,3,32,32]{3,2,1,0:T(8,128)S(1)} copy-done((f32[3,3,32,32]{3,2,1,0:T(8,128)S(1)}, f32[3,3,32,32]{3,2,1,0:T(8,128)}, u32[]{:S(2)}) %copy-start.1) | copy-done | bytes 36888
  4.6 0.8 %copy-done.2 = f32[3,3,8,32]{3,2,1,0:T(8,128)S(1)} copy-done((f32[3,3,8,32]{3,2,1,0:T(8,128)S(1)}, f32[3,3,8,32]{3,2,1,0:T(8,128)}, u32[]{:S(2)}) %copy-start.2) | copy-done | bytes 9240
  5.3 0.7 %copy-done.3 = f32[40,2,16,1]{0,3,2,1:T(1,128)S(1)} copy-done((f32[40,2,16,1]{0,3,2,1:T(1,128)S(1)}, f32[40,2,16,1]{0,3,2,1:T(1,128)}, u32[]{:S(2)}) %copy-start.3) | copy-done | bytes 5144
  6.1 0.7 %copy-done.4 = f32[2,16,128]{2,1,0:T(8,128)S(1)} copy-done((f32[2,16,128]{2,1,0:T(8,128)S(1)}, f32[2,16,128]{2,1,0:T(8,128)}, u32[]{:S(2)}) %copy-start.4) | copy-done | bytes 16408
  6.8 24.1 %shard_map.149 = (f32[2,16,128]{2,1,0:T(8,128)S(1)}, f32[16,128]{1,0:T(8,128)S(1)}) custom-call(bf16[40,2,16,128]{3,2,1,0:T(8,128)(2,1)S(1)} %copy-done, f32[2,16,1,40]{3,2,1,0:T(1,128)S(1)} %bitcast.6, f32[2,16,128]{2,1,0:T(8,128)S(1)} %copy-done.4, f32[1,1,128]{2,1,0:T(1,128)S(1)} %copy-done.5, f32[1,1,128]{2,1,0:T(1,128)S(1)} %copy-done.6, ...), custom_call_target="tpu_custom_call" | custom-call | tf_op jit(solution)/shard_map/pallas_call | solution.py:460
  30.9 0.6 %copy.20 = f32[2,16,128]{2,1,0:T(8,128)} copy(f32[2,16,128]{2,1,0:T(8,128)S(1)} %get-tuple-element.4) | data formatting | bytes 32768
  31.5 0.6 %copy.21 = f32[16,128]{1,0:T(8,128)} copy(f32[16,128]{1,0:T(8,128)S(1)} %get-tuple-element.5) | data formatting | bytes 16384
  (3 shorter events, 0.0 us)
Async XLA Ops:
  1.9 0.7 %copy-start.8 = (s32[1,1,128]{2,1,0:T(1,128)S(1)}, s32[1,1,128]{2,1,0:T(1,128)}, u32[]{:S(2)}) copy-start(s32[1,1,128]{2,1,0:T(1,128)} %level_ref.1) | copy-start | bytes 1540
  1.9 0.7 %copy-start.9 = (f32[32]{0:T(128)S(1)}, f32[32]{0:T(128)}, u32[]{:S(2)}) copy-start(f32[32]{0:T(128)} %param.23) | copy-start | bytes 388
  1.9 0.7 %copy-start.10 = (f32[32]{0:T(128)S(1)}, f32[32]{0:T(128)}, u32[]{:S(2)}) copy-start(f32[32]{0:T(128)} %param.25) | copy-start | bytes 388
  2.0 0.7 %copy-start.11 = (f32[32]{0:T(128)S(1)}, f32[32]{0:T(128)}, u32[]{:S(2)}) copy-start(f32[32]{0:T(128)} %param.26) | copy-start | bytes 388
  2.0 0.7 %copy-start.5 = (f32[1,1,128]{2,1,0:T(1,128)S(1)}, f32[1,1,128]{2,1,0:T(1,128)}, u32[]{:S(2)}) copy-start(f32[1,1,128]{2,1,0:T(1,128)} %values_ref.1) | copy-start | bytes 1540
  2.0 0.7 %copy-start.6 = (f32[1,1,128]{2,1,0:T(1,128)S(1)}, f32[1,1,128]{2,1,0:T(1,128)}, u32[]{:S(2)}) copy-start(f32[1,1,128]{2,1,0:T(1,128)} %error_ref.1) | copy-start | bytes 1540
  2.0 0.7 %copy-start.7 = (s32[1,1,128]{2,1,0:T(1,128)S(1)}, s32[1,1,128]{2,1,0:T(1,128)}, u32[]{:S(2)}) copy-start(s32[1,1,128]{2,1,0:T(1,128)} %cell_ref.1) | copy-start | bytes 1540
  2.7 1.0 %copy-start = (bf16[40,2,16,128]{3,2,1,0:T(8,128)(2,1)S(1)}, bf16[40,2,16,128]{3,2,1,0:T(8,128)(2,1)}, u32[]{:S(2)}) copy-start(bf16[40,2,16,128]{3,2,1,0:T(8,128)(2,1)} %codes_ref.1) | copy-start | bytes 983044
  3.7 0.9 %copy-start.1 = (f32[3,3,32,32]{3,2,1,0:T(8,128)S(1)}, f32[3,3,32,32]{3,2,1,0:T(8,128)}, u32[]{:S(2)}) copy-start(f32[3,3,32,32]{3,2,1,0:T(8,128)} %c2_ref.1) | copy-start | bytes 110596
  4.6 0.8 %copy-start.2 = (f32[3,3,8,32]{3,2,1,0:T(8,128)S(1)}, f32[3,3,8,32]{3,2,1,0:T(8,128)}, u32[]{:S(2)}) copy-start(f32[3,3,8,32]{3,2,1,0:T(8,128)} %c1_ref.1) | copy-start | bytes 27652
  5.3 0.7 %copy-start.3 = (f32[40,2,16,1]{0,3,2,1:T(1,128)S(1)}, f32[40,2,16,1]{0,3,2,1:T(1,128)}, u32[]{:S(2)}) copy-start(f32[40,2,16,1]{0,3,2,1:T(1,128)} %param.15) | copy-start | bytes 15364
  6.0 0.7 %copy-start.4 = (f32[2,16,128]{2,1,0:T(8,128)S(1)}, f32[2,16,128]{2,1,0:T(8,128)}, u32[]{:S(2)}) copy-start(f32[2,16,128]{2,1,0:T(8,128)} %back_ref.1) | copy-start | bytes 49156

commit v3 on v2

--- a/solution.py
+++ b/solution.py
@@ -38,20 +38,20 @@
     gxn,
     gyn,
     members,
-    codes_ref,
-    scale_ref,
-    back_ref,
-    values_ref,
-    error_ref,
-    cell_ref,
-    level_ref,
-    count_ref,
-    c1_ref,
-    c2_ref,
-    b1_ref,
-    b2_ref,
-    hw_ref,
-    hb_ref,
+    codes_hbm,
+    scale_hbm,
+    back_hbm,
+    values_hbm,
+    error_hbm,
+    cell_hbm,
+    level_hbm,
+    count_hbm,
+    c1_hbm,
+    c2_hbm,
+    b1_hbm,
+    b2_hbm,
+    hw_hbm,
+    hb_hbm,
     inc_ref,
     taper_ref,
     main,
@@ -70,12 +70,27 @@
     srecv,
     feat,
     hid,
-    near,
     coef,
     flat,
     scales,
     wtile,
     local,
+    rolled,
+    codes_ref,
+    scale_ref,
+    back_ref,
+    values_ref,
+    error_ref,
+    cell_ref,
+    level_ref,
+    count_ref,
+    c1_ref,
+    c2_ref,
+    b1_ref,
+    b2_ref,
+    hw_ref,
+    hb_ref,
+    in_sem,
     halo_send,
     halo_recv,
     obs_send,
@@ -97,6 +112,11 @@
     peer = (g, gx, gy, 1 - lev)
     first = (lev * 2).astype(F32)
 
+    hbm = (codes_hbm, scale_hbm, back_hbm, values_hbm, error_hbm, cell_hbm, level_hbm, count_hbm, c1_hbm, c2_hbm, b1_hbm, b2_hbm, hw_hbm, hb_hbm)
+    held = (codes_ref, scale_ref, back_ref, values_ref, error_ref, cell_ref, level_ref, count_ref, c1_ref, c2_ref, b1_ref, b2_ref, hw_ref, hb_ref)
+    fetch = [pltpu.make_async_copy(x, v, in_sem.at[k]) for k, (x, v) in enumerate(zip(hbm, held))]
+    for copy in fetch:
+        copy.start()
     barrier = pltpu.get_barrier_semaphore()
     pl.semaphore_signal(barrier, inc=1, device_id=peer, device_id_type=MESH)
     others = [(i, j) for i in range(gxn) for j in range(gyn) if (i, j) != (0, 0)]
@@ -170,6 +190,8 @@
             device_id_type=MESH,
         )
 
+    for copy in fetch:
+        copy.wait()
     for l in range(levs):
         for r in range(rows):
             scales[l * rows + r : l * rows + r + 1, 0:members] = scale_ref[l, r]
@@ -296,24 +318,21 @@
         ext[e, :, 0:cols] = main[e]
         spread_out = sum(dot(p, put, 0, 0) for p in split_two(erecv[e]))
         ext[e, :, cols:wide] = spread_out[0:both]
+        rolled[e] = pltpu.roll(ext[e], wide - STEP, 1)
 
     extent = rows + 2 * RIM
 
-    def row_sums(e, carry):
-        here = ext[e]
-        below = ext[jnp.minimum(e + STEP, extent - 1)]
-        terms = (
-            here * here,
-            here * pltpu.roll(below, STEP, 1),
-            here * below,
-            here * pltpu.roll(below, wide - STEP, 1),
-            here * pltpu.roll(here, wide - STEP, 1),
-        )
+    for e in range(extent):
+        here, here_next = ext[e], rolled[e]
+        terms = [here * here]
+        if e < extent - STEP:
+            below, below_next = ext[e + STEP], rolled[e + STEP]
+            terms += [here_next * below, here * below, here * below_next]
+        else:
+            terms += [jnp.zeros_like(here[0:8])] * 3
+        terms.append(here * here_next)
         for k, term in enumerate(terms):
-            sums[k, pl.ds(e, 1)] = jnp.sum(term, axis=0, keepdims=True)
-        return carry
-
-    lax.fori_loop(0, extent, row_sums, 0)
+            sums[k, e : e + 1] = jnp.sum(term, axis=0, keepdims=True)
     lev_sum = lev_copy(1, sums, speer)
     lev_sum.start()
     lev_sum.wait_recv()
@@ -321,6 +340,7 @@
     weight_total = float(members * total_levels)
     sq = (sums[0] + speer[0]) / weight_total + EPS
     q0, q1, q2, q3 = [(sums[k] + speer[k]) / weight_total for k in range(1, 5)]
+    q0 = pltpu.roll(q0, STEP, 1)
     top = extent - STEP
     s_here, s_below = sq[0:top], sq[STEP:extent]
     g0 = q0[0:top] / jnp.sqrt(s_here * pltpu.roll(s_below, STEP, 1))
@@ -341,23 +361,23 @@
     for k, channel in enumerate(channels):
         feat[:, k, :] = channel
 
-    def conv_row(x, wh, ws):
+    def conv_row(x, wh, ws, lanes):
         patch = jnp.concatenate([pltpu.roll(x, 1, 1), x, pltpu.roll(x, wide - 1, 1)], 0)
-        high, low = split_two(patch)
+        high, low = split_two(patch[:, 0:lanes])
         z = dot(ws, high)
         return z[0:96] + z[96:192] + dot(wh, low)
 
-    z1 = [conv_row(feat[i], w1h, w1s) for i in range(3)]
+    z1 = [conv_row(feat[i], w1h, w1s, wide) for i in range(3)]
     z2 = []
     tapers = []
     for i in range(rows + 2):
         h = z1[0][0:32] + z1[1][32:64] + z1[2][64:96]
         if i + 3 < rows + 4:
-            z1 = [z1[1], z1[2], conv_row(feat[i + 3], w1h, w1s)]
+            z1 = [z1[1], z1[2], conv_row(feat[i + 3], w1h, w1s, wide)]
         row_at = gx * rows + (i - 1)
         keep = col_in & (row_at >= 0) & (row_at < gxn * rows)
         h = jnp.where(keep, jnp.maximum(h + b1, 0.0), 0.0)
-        z2.append(conv_row(h, w2h, w2s)[:, 0:cols])
+        z2.append(conv_row(h, w2h, w2s, cols))
         if len(z2) == 3:
             out = z2[0][0:32] + z2[1][32:64] + z2[2][64:96]
             out = jnp.maximum(out + b2, 0.0)
@@ -384,23 +404,23 @@
     recv_all(obs_copy)
 
     tiles = [(tr, tc) for tr in (-1, 0, 1) for tc in (-1, 0, 1)]
-    row_list = []
+    def near_span(r):
+        return (0 if r < CUT - 1 else 3 * 128), (9 * 128 if r > rows - CUT else 6 * 128)
+
+    lanes = lax.broadcasted_iota(jnp.int32, (128, cols), 1).astype(F32)
     for t, (tr, tc) in enumerate(tiles):
         pack = opack if (tr, tc) == (0, 0) else orecv.at[MOVES.index((-tr, -tc))]
-        gap = y_sub - (pack[members + 4 : members + 5] + float(tc * cols))
-        near[:, t * 128 : t * 128 + 128] = gap * gap / float(CUT * CUT)
-        row_list.append(pack[members + 3 : members + 4] + float(tr * rows))
-    row_all = jnp.concatenate(row_list, 1)
-
-    def near_span(r):
-        return (0 if r < CUT - 1 else 3 * 128), (9 * 128 if r > rows - CUT else 6 * 128)
-
-    for r in range(rows):
-        k0, k1 = near_span(r)
-        gap = float(r) - row_all[:, k0:k1]
+        spots = pack[members : members + 8].T
+        gap = lanes - (spots[:, 4:5] + float(tc * cols))
+        near = gap * gap / float(CUT * CUT)
+        gap = lanes - (spots[:, 3:4] + float(tr * rows))
         base = 1.0 - gap * gap / float(CUT * CUT)
-        m = jnp.maximum(0.0, base - near[:, k0:k1])
-        local[r, :, 0 : k1 - k0] = (m * m).astype(BF16)
+        for r in range(rows):
+            if (tr == -1 and r >= CUT - 1) or (tr == 1 and r <= rows - CUT):
+                continue
+            m = jnp.maximum(0.0, base[:, r : r + 1] - near)
+            k0 = t * 128 - near_span(r)[0]
+            local[r, k0 : k0 + 128] = (m * m).astype(BF16)
     recv_all(wt_copy)
     for t, (tr, tc) in enumerate(tiles):
         d = None if (tr, tc) == (0, 0) else MOVES.index((-tr, -tc))
@@ -416,7 +436,7 @@
 
     for r in range(rows):
         k0, k1 = near_span(r)
-        w = dot(coef[:, k0:k1], local[r, :, 0 : k1 - k0], 1, 1)
+        w = dot(coef[:, k0:k1], local[r, 0 : k1 - k0])
         prod = main[RIM + r] * w
         scale = inflation * taper[r : r + 1]
         for l in range(2):
@@ -453,6 +473,22 @@
     both = members * levs
     scales = block_scales.transpose(1, 2, 3, 0)
     row = lambda v: v.reshape(1, -1)
+    args = (
+        anomaly_codes,
+        scales,
+        background,
+        obs_values,
+        obs_error,
+        obs_cell,
+        obs_level,
+        obs_count,
+        conv1_weight,
+        conv2_weight,
+        row(conv1_bias),
+        row(conv2_bias),
+        row(head_weight),
+        row(head_bias),
+    )
     vm = lambda *s, dtype=F32: pltpu.VMEM(s, dtype)
     sem = lambda n: pltpu.SemaphoreType.DMA((n,))
     extent = rows + 2 * RIM
@@ -463,7 +499,7 @@
             jax.ShapeDtypeStruct((levs, rows, cols), F32),
             jax.ShapeDtypeStruct((rows, cols), F32),
         ),
-        in_specs=[pl.BlockSpec(memory_space=pltpu.VMEM)] * 14,
+        in_specs=[pl.BlockSpec(memory_space=pltpu.HBM)] * len(args),
         out_specs=[pl.BlockSpec(memory_space=pltpu.VMEM)] * 2,
         scratch_shapes=[
             vm(extent, both, cols),
@@ -482,12 +518,14 @@
             vm(tiles, 8, 128),
             vm(rows + 4, 8, 2 * cols),
             vm(both, 9 * 128),
-            vm(cols, 9 * 128),
             vm(both, 9 * 128, dtype=BF16),
             vm(both * rows, cols),
             vm(128, 128),
             vm(128, 128),
-            vm(rows, cols, 6 * 128, dtype=BF16),
+            vm(rows, 6 * 128, cols, dtype=BF16),
+            vm(extent, both, 2 * cols),
+            *[vm(*x.shape, dtype=x.dtype) for x in args],
+            sem(len(args)),
             sem(8),
             sem(8),
             sem(8),
@@ -500,24 +538,9 @@
             sem(2),
         ],
         compiler_params=pltpu.CompilerParams(
-            collective_id=0, has_side_effects=True, vmem_limit_bytes=40 * 1024 * 1024
+            collective_id=0, has_side_effects=True, vmem_limit_bytes=62 * 1024 * 1024
         ),
-    )(
-        anomaly_codes,
-        scales,
-        background,
-        obs_values,
-        obs_error,
-        obs_cell,
-        obs_level,
-        obs_count,
-        conv1_weight,
-        conv2_weight,
-        row(conv1_bias),
-        row(conv2_bias),
-        row(head_weight),
-        row(head_bias),
-    )
+    )(*args)
 
 
 def solution(mesh):

time: 32.5 us -> 25.7 us (0.79)
  local copies, waits for them, and re-layouts: 5.98 us -> 1.93 us
  Pallas kernels: 24.1 us -> 21.6 us
    unnamed x26 -> x4, local copies, waits for them, and re-layouts: 5.98 us -> 1.93 us
    pallas_call x1, Pallas kernels: 24.1 us -> 21.6 us  [per_device(): pl.pallas_call(functools.partial(kernel, gxn, gyn, members), out_shape=(j...]
where the time goes in v3:
time: 25.7 us; the launch traced here: 25.5 us
  Pallas kernels  21.6 us (84%)
  between operations  1.94 us (8%)
  local copies, waits for them, and re-layouts  1.93 us (8%)
    pallas_call x1, Pallas kernels, per_device(): pl.pallas_call(functools.partial(kernel, gxn, gyn, members), out_shape=(j...  21.6 us
    unnamed x4, local copies, waits for them, and re-layouts  1.93 us

profile of v3, /device:TPU:0, one launch (start us, length us, event | category | flops | bytes accessed | tf_op | source)
XLA Modules:
  0.0 25.5 jit_solution(15258465729313327589)
XLA Ops:
  1.9 21.6 %shard_map.149 = (f32[2,16,128]{2,1,0:T(8,128)}, f32[16,128]{1,0:T(8,128)}) custom-call(bf16[40,2,16,128]{3,2,1,0:T(8,128)(2,1)} %codes_hbm.1, f32[2,16,1,40]{3,2,1,0:T(1,128)} %bitcast.6, f32[2,16,128]{2,1,0:T(8,128)} %back_hbm.1, f32[1,1,128]{2,1,0:T(1,128)} %values_hbm.1, f32[1,1,128]{2,1,0:T(1,128)} %error_hbm.1, s32[1,1,128]{2,1,0:T(1,128)} %cell_hbm.1, ...), custom_call_target="tpu_custom_call" | custom-call | tf_op jit(solution)/shard_map/pallas_call | solution.py:496
  23.6 0.0 copy-start
  23.6 1.3 %copy.20 = f32[2,16,128]{2,1,0:T(8,128)} copy(f32[2,16,128]{2,1,0:T(8,128)} %get-tuple-element.4) | data formatting | bytes 32768
  24.9 0.0 copy-done
  24.9 0.6 %copy.21 = f32[16,128]{1,0:T(8,128)} copy(f32[16,128]{1,0:T(8,128)S(1)} %copy-done) | data formatting | bytes 16384
Async XLA Ops:
  23.6 1.3 %copy-start = (f32[16,128]{1,0:T(8,128)S(1)}, f32[16,128]{1,0:T(8,128)}, u32[]{:S(2)}) copy-start(f32[16,128]{1,0:T(8,128)} %get-tuple-element.5) | copy-start | bytes 24580

commit v4 on v3

--- a/solution.py
+++ b/solution.py
@@ -165,12 +165,14 @@
             device_id_type=MESH,
         )
 
-    def start_all(copy):
-        for d, (dr, dc) in enumerate(MOVES):
+    def start_all(copy, moves=range(8)):
+        for d in moves:
+            dr, dc = MOVES[d]
             pl.when(exists(dr, dc))(lambda d=d: copy(d).start())
 
-    def recv_all(copy):
-        for d, (dr, dc) in enumerate(MOVES):
+    def recv_all(copy, moves=range(8)):
+        for d in moves:
+            dr, dc = MOVES[d]
             pl.when(exists(-dr, -dc))(lambda d=d: copy(d).wait_recv())
 
     def sent_all(copy):
@@ -219,12 +221,16 @@
             orecv[d] = jnp.zeros(orecv.shape[1:], F32)
             wrecv[d] = jnp.zeros(wrecv.shape[1:], F32)
 
+    pl.semaphore_wait(barrier, gxn * gyn)
+    start_all(halo_copy, (1, 6))
+
     c8 = lax.broadcasted_iota(jnp.int32, (8, cols), 0)
     j8 = lax.broadcasted_iota(jnp.int32, (8, cols), 1)
     pick = (j8 == jnp.where(c8 < RIM, c8, cols - 8 + c8)).astype(F32).astype(BF16)
     ecol[...] = jnp.zeros(ecol.shape, F32)
     for r in range(rows):
         ecol[r, :, 0:both] = sum(dot(pick, p, 1, 1) for p in split_two(main[RIM + r]))
+    start_all(halo_copy, (3, 4, 0, 2, 5, 7))
 
     cell = cell_ref[0]
     level = level_ref[0].astype(F32)
@@ -233,9 +239,6 @@
     error = error_ref[0]
     y_sub = lax.broadcasted_iota(jnp.int32, (cols, 128), 0).astype(F32)
     onehot = (y_sub == col_o).astype(F32).astype(BF16)
-
-    pl.semaphore_wait(barrier, gxn * gyn)
-    start_all(halo_copy)
 
     mine = jnp.zeros((members, 128), F32)
     for r in range(rows):
@@ -307,22 +310,22 @@
     for k in range(len(others)):
         stat_copy(k).start()
 
-    recv_all(halo_copy)
+    recv_all(halo_copy, (3, 4))
 
     c16 = lax.broadcasted_iota(jnp.int32, (16, cols), 0)
     j16 = lax.broadcasted_iota(jnp.int32, (16, cols), 1)
     put = (
         ((j16 < RIM) & (c16 == j16 + 8)) | ((j16 >= cols - RIM) & (c16 == j16 - (cols - 8)))
     ).astype(F32).astype(BF16)
-    for e in range(rows + 2 * RIM):
+    extent = rows + 2 * RIM
+
+    def widen(e):
         ext[e, :, 0:cols] = main[e]
         spread_out = sum(dot(p, put, 0, 0) for p in split_two(erecv[e]))
         ext[e, :, cols:wide] = spread_out[0:both]
         rolled[e] = pltpu.roll(ext[e], wide - STEP, 1)
 
-    extent = rows + 2 * RIM
-
-    for e in range(extent):
+    def row_sums(e):
         here, here_next = ext[e], rolled[e]
         terms = [here * here]
         if e < extent - STEP:
@@ -333,6 +336,18 @@
         terms.append(here * here_next)
         for k, term in enumerate(terms):
             sums[k, e : e + 1] = jnp.sum(term, axis=0, keepdims=True)
+
+    inner = list(range(RIM, RIM + rows))
+    for e in inner:
+        widen(e)
+    for e in inner[:-STEP]:
+        row_sums(e)
+    recv_all(halo_copy, (0, 1, 2, 5, 6, 7))
+    rim = [e for e in range(extent) if e not in inner]
+    for e in rim:
+        widen(e)
+    for e in rim + inner[-STEP:]:
+        row_sums(e)
     lev_sum = lev_copy(1, sums, speer)
     lev_sum.start()
     lev_sum.wait_recv()
@@ -441,7 +456,7 @@
         scale = inflation * taper[r : r + 1]
         for l in range(2):
             part = jnp.sum(prod[l * members : (l + 1) * members], axis=0, keepdims=True)
-            inc_ref[l, r : r + 1] = scale * part
+            inc_ref[l * rows + r : l * rows + r + 1] = scale * part
 
     sent_all(halo_copy)
     sent_all(obs_copy)
@@ -493,10 +508,10 @@
     sem = lambda n: pltpu.SemaphoreType.DMA((n,))
     extent = rows + 2 * RIM
     tiles = gxn * gyn - 1
-    return pl.pallas_call(
+    inc, taper = pl.pallas_call(
         functools.partial(kernel, gxn, gyn, members),
         out_shape=(
-            jax.ShapeDtypeStruct((levs, rows, cols), F32),
+            jax.ShapeDtypeStruct((levs * rows, cols), F32),
             jax.ShapeDtypeStruct((rows, cols), F32),
         ),
         in_specs=[pl.BlockSpec(memory_space=pltpu.HBM)] * len(args),
@@ -541,6 +556,7 @@
             collective_id=0, has_side_effects=True, vmem_limit_bytes=62 * 1024 * 1024
         ),
     )(*args)
+    return inc.reshape(levs, rows, cols), taper
 
 
 def solution(mesh):

time: 25.7 us -> 25.1 us (0.977)
  Pallas kernels: 21.6 us -> 21 us
    pallas_call x1, Pallas kernels: 21.6 us -> 21 us  [per_device(): pl.pallas_call(functools.partial(kernel, gxn, gyn, members), out_shape=(j...]
where the time goes in v4:
time: 25.1 us; the launch traced here: 24.8 us
  Pallas kernels  21 us (84%)
  between operations  1.94 us (8%)
  local copies, waits for them, and re-layouts  1.93 us (8%)
    pallas_call x1, Pallas kernels, per_device(): pl.pallas_call(functools.partial(kernel, gxn, gyn, members), out_shape=(j...  21 us
    unnamed x4, local copies, waits for them, and re-layouts  1.93 us

profile of v4, /device:TPU:0, one launch (start us, length us, event | category | flops | bytes accessed | tf_op | source)
XLA Modules:
  0.0 24.8 jit_solution(4144343108287805399)
XLA Ops:
  1.9 21.0 %shard_map.149 = (f32[32,128]{1,0:T(8,128)}, f32[16,128]{1,0:T(8,128)}) custom-call(bf16[40,2,16,128]{3,2,1,0:T(8,128)(2,1)} %codes_hbm.1, f32[2,16,1,40]{3,2,1,0:T(1,128)} %bitcast.7, f32[2,16,128]{2,1,0:T(8,128)} %back_hbm.1, f32[1,1,128]{2,1,0:T(1,128)} %values_hbm.1, f32[1,1,128]{2,1,0:T(1,128)} %error_hbm.1, s32[1,1,128]{2,1,0:T(1,128)} %cell_hbm.1, ...), custom_call_target="tpu_custom_call" | custom-call | tf_op jit(solution)/shard_map/pallas_call | solution.py:511
  22.9 0.0 copy-start
  22.9 1.3 %copy.20 = f32[2,16,128]{2,1,0:T(8,128)} copy(f32[2,16,128]{2,1,0:T(8,128)} %bitcast.8) | data formatting | bytes 32768
  24.2 0.0 copy-done
  24.2 0.6 %copy.21 = f32[16,128]{1,0:T(8,128)} copy(f32[16,128]{1,0:T(8,128)S(1)} %copy-done) | data formatting | bytes 16384
Async XLA Ops:
  22.9 1.3 %copy-start = (f32[16,128]{1,0:T(8,128)S(1)}, f32[16,128]{1,0:T(8,128)}, u32[]{:S(2)}) copy-start(f32[16,128]{1,0:T(8,128)} %get-tuple-element.9) | copy-start | bytes 24580

commit v5 on v4

--- a/solution.py
+++ b/solution.py
@@ -350,6 +350,31 @@
         row_sums(e)
     lev_sum = lev_copy(1, sums, speer)
     lev_sum.start()
+    recv_all(obs_copy)
+
+    tiles = [(tr, tc) for tr in (-1, 0, 1) for tc in (-1, 0, 1)]
+    def near_span(r):
+        return (0 if r < CUT - 1 else 3 * 128), (9 * 128 if r > rows - CUT else 6 * 128)
+
+    lanes = lax.broadcasted_iota(jnp.int32, (128, cols), 1).astype(F32)
+    def localize(which):
+      for t, (tr, tc) in enumerate(tiles):
+        if tr not in which:
+            continue
+        pack = opack if (tr, tc) == (0, 0) else orecv.at[MOVES.index((-tr, -tc))]
+        spots = pack[members : members + 8].T
+        gap = lanes - (spots[:, 4:5] + float(tc * cols))
+        near = gap * gap / float(CUT * CUT)
+        gap = lanes - (spots[:, 3:4] + float(tr * rows))
+        base = 1.0 - gap * gap / float(CUT * CUT)
+        for r in range(rows):
+            if (tr == -1 and r >= CUT - 1) or (tr == 1 and r <= rows - CUT):
+                continue
+            m = jnp.maximum(0.0, base[:, r : r + 1] - near)
+            k0 = t * 128 - near_span(r)[0]
+            local[r, k0 : k0 + 128] = (m * m).astype(BF16)
+
+    localize((0,))
     lev_sum.wait_recv()
 
     weight_total = float(members * total_levels)
@@ -416,26 +441,7 @@
     weight = at_obs * gain / (members - 1)
     wown[...] = jnp.broadcast_to(weight, (8, 128))
     start_all(wt_copy)
-    recv_all(obs_copy)
-
-    tiles = [(tr, tc) for tr in (-1, 0, 1) for tc in (-1, 0, 1)]
-    def near_span(r):
-        return (0 if r < CUT - 1 else 3 * 128), (9 * 128 if r > rows - CUT else 6 * 128)
-
-    lanes = lax.broadcasted_iota(jnp.int32, (128, cols), 1).astype(F32)
-    for t, (tr, tc) in enumerate(tiles):
-        pack = opack if (tr, tc) == (0, 0) else orecv.at[MOVES.index((-tr, -tc))]
-        spots = pack[members : members + 8].T
-        gap = lanes - (spots[:, 4:5] + float(tc * cols))
-        near = gap * gap / float(CUT * CUT)
-        gap = lanes - (spots[:, 3:4] + float(tr * rows))
-        base = 1.0 - gap * gap / float(CUT * CUT)
-        for r in range(rows):
-            if (tr == -1 and r >= CUT - 1) or (tr == 1 and r <= rows - CUT):
-                continue
-            m = jnp.maximum(0.0, base[:, r : r + 1] - near)
-            k0 = t * 128 - near_span(r)[0]
-            local[r, k0 : k0 + 128] = (m * m).astype(BF16)
+    localize((-1, 1))
     recv_all(wt_copy)
     for t, (tr, tc) in enumerate(tiles):
         d = None if (tr, tc) == (0, 0) else MOVES.index((-tr, -tc))

time: 25.1 us -> 26.2 us (1.044)
  Pallas kernels: 21 us -> 22.2 us
    pallas_call x1, Pallas kernels: 21 us -> 22.2 us  [per_device(): pl.pallas_call(functools.partial(kernel, gxn, gyn, members), out_shape=(j...]
where the time goes in v5:
time: 26.2 us; the launch traced here: 26 us
  Pallas kernels  22.2 us (85%)
  between operations  1.94 us (7%)
  local copies, waits for them, and re-layouts  1.93 us (7%)
    pallas_call x1, Pallas kernels, per_device(): pl.pallas_call(functools.partial(kernel, gxn, gyn, members), out_shape=(j...  22.2 us
    unnamed x4, local copies, waits for them, and re-layouts  1.93 us

profile of v5, /device:TPU:0, one launch (start us, length us, event | category | flops | bytes accessed | tf_op | source)
XLA Modules:
  0.0 26.0 jit_solution(6664533343636101704)
XLA Ops:
  1.9 22.2 %shard_map.149 = (f32[32,128]{1,0:T(8,128)}, f32[16,128]{1,0:T(8,128)}) custom-call(bf16[40,2,16,128]{3,2,1,0:T(8,128)(2,1)} %codes_hbm.1, f32[2,16,1,40]{3,2,1,0:T(1,128)} %bitcast.7, f32[2,16,128]{2,1,0:T(8,128)} %back_hbm.1, f32[1,1,128]{2,1,0:T(1,128)} %values_hbm.1, f32[1,1,128]{2,1,0:T(1,128)} %error_hbm.1, s32[1,1,128]{2,1,0:T(1,128)} %cell_hbm.1, ...), custom_call_target="tpu_custom_call" | custom-call | tf_op jit(solution)/shard_map/pallas_call | solution.py:517
  24.1 0.0 copy-start
  24.1 1.3 %copy.20 = f32[2,16,128]{2,1,0:T(8,128)} copy(f32[2,16,128]{2,1,0:T(8,128)} %bitcast.8) | data formatting | bytes 32768
  25.4 0.0 copy-done
  25.4 0.6 %copy.21 = f32[16,128]{1,0:T(8,128)} copy(f32[16,128]{1,0:T(8,128)S(1)} %copy-done) | data formatting | bytes 16384
Async XLA Ops:
  24.1 1.3 %copy-start = (f32[16,128]{1,0:T(8,128)S(1)}, f32[16,128]{1,0:T(8,128)}, u32[]{:S(2)}) copy-start(f32[16,128]{1,0:T(8,128)} %get-tuple-element.9) | copy-start | bytes 24580
